TPU v7x, 512 devices: a whole 4x4x16 slice. The times are simulated.
512 devices in a mesh: dom: 512 (over x, z, y, core).
Axes of the slice: x: 4, y: 4, z: 16, core: 2. Of those that a mesh axis runs over, the one named last changes fastest.
Arguments:
- x_block: float32 [16, 16, 65536], P(None, None, 'dom'), may hold values from -37 to 37
- p_block: float32 [16, 16, 65536], P(None, None, 'dom'), may hold values from -46 to 46
- f_own: float32 [4, 16, 16, 65536], P(None, None, None, 'dom'), may hold values from -0.75 to 0.75
- f_other: float32 [4, 16, 16, 65536], P(None, None, None, 'dom'), may hold values from -0.75 to 0.75
- node_mass: float32 [16, 65536], P(None, 'dom'), may hold values from 0.5 to 6
- block_cols: int32 [4, 65536], P(None, 'dom'), may hold values from 0 to 159, as said below
- degree: int32 [65536], P('dom'), may hold values from 1 to 4, as said below
- send_list: int32 [16384], P('dom'), may hold values from 0 to 127, as said below
- pair_list: int32 [16384], P('dom'), may hold values from 0 to 127, as said below
- partner: int32 [65536], P('dom'), may hold values from 0 to 159, as said below
Outputs:
- precond: float32 [16, 16, 65536], P(None, None, 'dom')
- gram_a: float32 [48, 48], replicated
- gram_b: float32 [48, 48], replicated
Inputs may be any that keep to these rules, and one draw needn't show every extreme that they name: `block_cols`: per partition, slot 0 is live on every row; entries never name the row itself; every extended index from 128 to 159 is named by some slot 0 of each partition. `degree`: some row of every partition has all 4 slots live. `send_list`: per partition 2 * 16 distinct local nodes. `pair_list`: per partition 2 * 16 distinct local nodes. Pairing is symmetric and covers every node once: a local partner's partner is the node itself, node pair_list[j] of a partition has partner 128 + j, and the lower neighbour's pair_list[16 + i] is paired with this partition's pair_list[i].
All inputs are finite; a program needn't handle non-finite values.
Results may differ from a plain program's by a relative error of at most 0.0003.
Values sent between devices are 32-bit elements; how exact they have to be, the bound alone decides.
A program may use at most 64 MiB of HBM per device.

v0:
```python
import jax
import jax.numpy as jnp
from jax import lax
from jax.sharding import PartitionSpec as P

smooth_weight = 0.5
coarse_weight = 0.5
highest = lax.Precision.HIGHEST


def extended_2(shard, sides, width):
    for axis, dim in sides:
        devices, length = (lax.axis_size(axis), shard.shape[dim])
        up = [(i, (i + 1) % devices) for i in range(devices)]
        down = [(j, i) for i, j in up]
        last = lax.slice_in_dim(shard, length - width, length, axis=dim)
        first = lax.slice_in_dim(shard, 0, width, axis=dim)
        before = lax.ppermute(last, axis, up)
        after = lax.ppermute(first, axis, down)
        shard = jnp.concatenate([before, shard, after], axis=dim)
    return shard


def slot_mask(block_cols, degree):
    slot_index = lax.broadcasted_iota(jnp.int32, block_cols.shape, 0)
    return (slot_index < degree[None, :]).astype(jnp.float32)


def edge_terms(extended, local_vec, f_own, f_other, block_cols, live_slots):
    remote = jnp.moveaxis(jnp.take(extended, block_cols, axis=2), 2, 0)
    own_map = jnp.sum(f_own[:, :, :, None, :] * local_vec[None, None, :, :, :], axis=2)
    far_map = jnp.sum(f_other[:, :, :, None, :] * remote[:, None, :, :, :], axis=2)
    mismatch = (own_map - far_map) * live_slots[:, None, None, :]
    own_part = jnp.sum(f_own[:, :, :, None, :] * mismatch[:, :, None, :, :], axis=(0, 1))
    far_part = jnp.sum(f_other[:, :, :, None, :] * mismatch[:, :, None, :, :], axis=1)
    node_count = local_vec.shape[2]
    gathered = (
        jnp.zeros(extended.shape, jnp.float32)
        .at[:, :, block_cols]
        .add(-jnp.moveaxis(far_part, 0, 2))
    )
    return (own_part + gathered[:, :, :node_count], gathered[:, :, node_count:])


def diagonal_terms(f_own, f_other, block_cols, live_slots, extended_len):
    live_wide = live_slots[:, None, None, :]
    own_square = jnp.sum(f_own * f_own * live_wide, axis=(0, 1))
    far_square = jnp.moveaxis(jnp.sum(f_other * f_other * live_wide, axis=1), 0, 1)
    node_count = block_cols.shape[1]
    gathered = (
        jnp.zeros((far_square.shape[0], extended_len), jnp.float32)
        .at[:, block_cols]
        .add(far_square)
    )
    return (own_square + gathered[:, :node_count], gathered[:, node_count:])


def solve_spd(matrix, rhs_matrix):
    factor = jnp.linalg.cholesky(matrix)
    middle = lax.linalg.triangular_solve(factor, rhs_matrix, left_side=True, lower=True)
    return lax.linalg.triangular_solve(factor, middle, left_side=True, lower=True, transpose_a=True)


def gram_block(left, right, norm_scale):
    return jnp.einsum("scn,sen->ce", left, right, precision=highest) * norm_scale


def shards(
    x_block, p_block, f_own, f_other, node_mass, block_cols, degree, send_list, pair_list, partner
):
    stalk_size = x_block.shape[0]
    columns = x_block.shape[1]
    node_count = x_block.shape[2]
    half_halo = send_list.shape[0] // 2
    half_pair = pair_list.shape[0] // 2
    norm_scale = 1.0 / (node_count * stalk_size * lax.axis_size("dom"))
    live_slots = slot_mask(block_cols, degree)

    def extend(vectors):
        packed = vectors[:, :, send_list]
        received = extended_2(packed, (("dom", 2),), half_halo)
        return jnp.concatenate(
            [vectors, received[:, :, :half_halo], received[:, :, 3 * half_halo :]], axis=2
        )

    def returned(payload):
        received = extended_2(payload, (("dom", 2),), half_halo)
        return jnp.concatenate(
            [received[:, :, :half_halo], received[:, :, 3 * half_halo :]], axis=2
        )

    def partner_sum(vectors):
        packed = vectors[:, :, pair_list]
        received = extended_2(packed, (("dom", 2),), half_pair)
        extended = jnp.concatenate(
            [vectors, received[:, :, :half_pair], received[:, :, 3 * half_pair :]], axis=2
        )
        return vectors + jnp.take(extended, partner, axis=2)

    def operator(vectors):
        inner_part, outgoing = edge_terms(
            extend(vectors), vectors, f_own, f_other, block_cols, live_slots
        )
        result = inner_part + node_mass[:, None, :] * vectors
        return result.at[:, :, send_list].add(returned(outgoing))

    stacked = jnp.concatenate([x_block, p_block], axis=1)
    inner_part, outgoing = edge_terms(
        extend(stacked), stacked, f_own, f_other, block_cols, live_slots
    )
    diag_inner, diag_out = diagonal_terms(
        f_own, f_other, block_cols, live_slots, node_count + 2 * half_halo
    )
    incoming = returned(jnp.concatenate([outgoing, diag_out[:, None, :]], axis=1))
    applied = (
        (inner_part + node_mass[:, None, :] * stacked)
        .at[:, :, send_list]
        .add(incoming[:, : 2 * columns])
    )
    diagonal = (node_mass + diag_inner).at[:, send_list].add(incoming[:, 2 * columns])
    image_x = applied[:, :columns]
    image_p = applied[:, columns:]
    gram_xx, gram_xa = lax.psum(
        (gram_block(x_block, x_block, norm_scale), gram_block(x_block, image_x, norm_scale)), "dom"
    )
    quotient = solve_spd(gram_xx, gram_xa)
    residual = image_x - jnp.einsum("scn,ce->sen", x_block, quotient, precision=highest)
    breadth = residual.shape[1]
    inverse = 1.0 / diagonal[:, None, :]
    correction = smooth_weight * residual * inverse
    correction = correction + smooth_weight * (residual - operator(correction)) * inverse
    leftover = residual - operator(correction)
    summed = partner_sum(jnp.concatenate([leftover, diagonal[:, None, :]], axis=1))
    coarse_rhs = summed[:, :breadth]
    coarse_diag = summed[:, breadth:]
    coarse = coarse_weight * coarse_rhs / coarse_diag
    coarse = coarse + coarse_weight * (coarse_rhs - partner_sum(operator(coarse))) / coarse_diag
    correction = correction + coarse
    correction = correction + smooth_weight * (residual - operator(correction)) * inverse
    correction = correction + smooth_weight * (residual - operator(correction)) * inverse
    image_w = operator(correction)
    basis = jnp.concatenate([x_block, correction, p_block], axis=1)
    images = jnp.concatenate([image_x, image_w, image_p], axis=1)
    gram_a, gram_b = lax.psum(
        (gram_block(basis, images, norm_scale), gram_block(basis, basis, norm_scale)), "dom"
    )
    return (correction, gram_a, gram_b)


def solution(mesh):
    return jax.shard_map(
        shards,
        mesh=mesh,
        in_specs=(
            P(None, None, "dom"),
            P(None, None, "dom"),
            P(None, None, None, "dom"),
            P(None, None, None, "dom"),
            P(None, "dom"),
            P(None, "dom"),
            P("dom"),
            P("dom"),
            P("dom"),
            P("dom"),
        ),
        out_specs=(P(None, None, "dom"), P(), P()),
        check_vma=False,
    )
```

profile of v0, /device:TPU:1, one launch (start us, length us, event | category | flops | bytes accessed | tf_op | source)
XLA Modules:
  0.0 914.5 jit_solution(8142559367289408151)
XLA Ops:
  5.1 4.6 collective-permute-start
  9.7 6.1 collective-permute-start.1
  19.1 3.8 multiply_reduce_fusion.3
  28.9 3.1 gather_fusion.1
  32.0 3.9 select_bitcast_fusion.6
  35.9 3.1 copy.408
  40.9 4.2 multiply_reduce_fusion
  48.1 40.1 %scatter_fusion = f32[16,32,160]{1,0,2:T(8,128)S(1)} fusion(f32[16,32,160]{1,0,2:T(8,128)S(1)} %broadcast_in_dim.55, s32[512]{0:T(512)S(1)} %fusion.27, f32[512,16,32]{2,1,0:T(8,128)} %bitcast.155), kind=kCustom, calls=%fused_computation.18 | custom fusion | flops 262144 | bytes 3147776 | tf_op jit(solution)/shard_map/scatter-add | solution.py:40
  92.1 10.1 %collective-permute-start.3 = (f32[16,33,16]{1,0,2:T(8,128)}, f32[16,33,16]{1,0,2:T(8,128)}, u32[]{:S(2)}, u32[]{:S(2)}) collective-permute-start(f32[16,33,16]{1,0,2:T(8,128)} %get-tuple-element.38), channel_id=1, source_target_pairs={{1,0},{2,1},{3,2},{4,3},{5,4},{6,5},{7,6},{8,7},{9,8},{10,9},{11,1... | collective-permute-start | bytes 101384 | tf_op jit(solution)/shard_map/ppermute | solution.py:19
  110.7 110.6 %all-reduce.1 = (f32[16,16]{1,0:T(8,128)S(1)}, f32[16,16]{0,1:T(8,128)S(1)}) all-reduce(f32[16,16]{1,0:T(8,128)S(1)} %fusion.4, f32[16,16]{0,1:T(8,128)S(1)} %fusion.5), channel_id=1, replica_groups=mesh['dom'=512] {'dom'}, use_global_device_ids=true, to_apply=%region_11.12 | all-reduce | flops 512 | bytes 4096 | tf_op jit(solution)/shard_map/psum | solution.py:123
  238.5 3.1 gather_fusion.12
  241.6 3.9 select_bitcast_fusion.5
  245.5 3.1 copy.430
  253.9 40.1 %scatter_fusion.2 = f32[16,16,160]{1,0,2:T(8,128)S(1)} fusion(f32[16,16,160]{1,0,2:T(8,128)S(1)} %broadcast.159.clone, s32[512]{0:T(512)S(1)} %fusion.27, f32[512,16,16]{2,1,0:T(8,128)} %bitcast.159), kind=kCustom, calls=%fused_computation.22 | custom fusion | flops 131072 | bytes 1574912 | tf_op jit(solution)/shard_map/scatter-add | solution.py:40
  297.1 8.2 collective-permute-start.7
  312.9 9.8 %collective-permute-start.9 = (f32[16,16,16]{2,1,0:T(8,128)S(1)}, f32[16,16,16]{2,1,0:T(8,128)S(1)}, u32[]{:S(2)}, u32[]{:S(2)}) collective-permute-start(f32[16,16,16]{2,1,0:T(8,128)S(1)} %get-tuple-element.55), channel_id=1, source_target_pairs={{1,0},{2,1},{3,2},{4,3},{5,4},{6,5},{7,6},{8,7},{9,8},{10,9},{11,1... | collective-permute-start | bytes 49160 | tf_op jit(solution)/shard_map/ppermute | solution.py:19
  324.9 3.1 gather_fusion.13
  328.0 3.9 select_bitcast_fusion.4
  331.9 3.0 copy.439
  341.3 40.1 %scatter_fusion.4 = f32[16,16,160]{1,0,2:T(8,128)S(1)} fusion(f32[16,16,160]{1,0,2:T(8,128)S(1)} %broadcast.159.clone.1, s32[512]{0:T(512)S(1)} %fusion.27, f32[512,16,16]{2,1,0:T(8,128)} %bitcast.160), kind=kCustom, calls=%fused_computation.24 | custom fusion | flops 131072 | bytes 1574912 | tf_op jit(solution)/shard_map/scatter-add | solution.py:40
  385.1 9.9 %collective-permute-start.11 = (f32[16,16,16]{1,0,2:T(8,128)S(1)}, f32[16,16,16]{1,0,2:T(8,128)}, u32[]{:S(2)}, u32[]{:S(2)}) collective-permute-start(f32[16,16,16]{1,0,2:T(8,128)S(1)} %get-tuple-element.33), channel_id=1, source_target_pairs={{1,0},{2,1},{3,2},{4,3},{5,4},{6,5},{7,6},{8,7},{9,8},{10,9},{11,1... | collective-permute-start | bytes 49160 | tf_op jit(solution)/shard_map/ppermute | solution.py:19
  403.7 9.5 %collective-permute-start.13 = (f32[16,17,16]{2,1,0:T(8,128)S(1)}, f32[16,17,16]{2,1,0:T(8,128)S(1)}, u32[]{:S(2)}, u32[]{:S(2)}) collective-permute-start(f32[16,17,16]{2,1,0:T(8,128)S(1)} %get-tuple-element.45), channel_id=1, source_target_pairs={{1,0},{2,1},{3,2},{4,3},{5,4},{6,5},{7,6},{8,7},{9,8},{10,9},{11,1... | collective-permute-start | bytes 52232 | tf_op jit(solution)/shard_map/ppermute | solution.py:19
  421.8 11.8 %collective-permute-start.15 = (f32[16,16,16]{2,1,0:T(8,128)S(1)}, f32[16,16,16]{2,1,0:T(8,128)S(1)}, u32[]{:S(2)}, u32[]{:S(2)}) collective-permute-start(f32[16,16,16]{2,1,0:T(8,128)S(1)} %get-tuple-element.53), channel_id=1, source_target_pairs={{1,0},{2,1},{3,2},{4,3},{5,4},{6,5},{7,6},{8,7},{9,8},{10,9},{11,1... | collective-permute-start | bytes 49160 | tf_op jit(solution)/shard_map/ppermute | solution.py:19
  437.6 3.1 gather_fusion.14
  440.7 3.9 select_bitcast_fusion.3
  444.6 3.0 copy.453
  454.0 40.1 %scatter_fusion.6 = f32[16,16,160]{1,0,2:T(8,128)S(1)} fusion(f32[16,16,160]{1,0,2:T(8,128)S(1)} %broadcast.159.clone.2, s32[512]{0:T(512)S(1)} %fusion.27, f32[512,16,16]{2,1,0:T(8,128)} %bitcast.161), kind=kCustom, calls=%fused_computation.26 | custom fusion | flops 131072 | bytes 1574912 | tf_op jit(solution)/shard_map/scatter-add | solution.py:40
  497.8 9.8 %collective-permute-start.17 = (f32[16,16,16]{1,0,2:T(8,128)}, f32[16,16,16]{1,0,2:T(8,128)}, u32[]{:S(2)}, u32[]{:S(2)}) collective-permute-start(f32[16,16,16]{1,0,2:T(8,128)} %get-tuple-element.31), channel_id=1, source_target_pairs={{1,0},{2,1},{3,2},{4,3},{5,4},{6,5},{7,6},{8,7},{9,8},{10,9},{11,1... | collective-permute-start | bytes 49160 | tf_op jit(solution)/shard_map/ppermute | solution.py:19
  516.3 9.2 %collective-permute-start.19 = (f32[16,16,16]{1,0,2:T(8,128)}, f32[16,16,16]{1,0,2:T(8,128)S(1)}, u32[]{:S(2)}, u32[]{:S(2)}) collective-permute-start(f32[16,16,16]{1,0,2:T(8,128)} %get-tuple-element.41), channel_id=1, source_target_pairs={{1,0},{2,1},{3,2},{4,3},{5,4},{6,5},{7,6},{8,7},{9,8},{10,9},{11,1... | collective-permute-start | bytes 49160 | tf_op jit(solution)/shard_map/ppermute | solution.py:19
  535.1 9.5 %collective-permute-start.21 = (f32[16,16,16]{2,1,0:T(8,128)S(1)}, f32[16,16,16]{2,1,0:T(8,128)S(1)}, u32[]{:S(2)}, u32[]{:S(2)}) collective-permute-start(f32[16,16,16]{2,1,0:T(8,128)S(1)} %get-tuple-element.51), channel_id=1, source_target_pairs={{1,0},{2,1},{3,2},{4,3},{5,4},{6,5},{7,6},{8,7},{9,8},{10,9},{11,1... | collective-permute-start | bytes 49160 | tf_op jit(solution)/shard_map/ppermute | solution.py:19
  547.0 3.1 gather_fusion.15
  550.0 3.9 select_bitcast_fusion.2
  553.9 3.0 copy.463
  563.4 40.1 %scatter_fusion.8 = f32[16,16,160]{1,0,2:T(8,128)S(1)} fusion(f32[16,16,160]{1,0,2:T(8,128)S(1)} %broadcast.159.clone.3, s32[512]{0:T(512)S(1)} %fusion.27, f32[512,16,16]{2,1,0:T(8,128)} %bitcast.162), kind=kCustom, calls=%fused_computation.28 | custom fusion | flops 131072 | bytes 1574912 | tf_op jit(solution)/shard_map/scatter-add | solution.py:40
  607.1 9.8 %collective-permute-start.23 = (f32[16,16,16]{1,0,2:T(8,128)S(1)}, f32[16,16,16]{1,0,2:T(8,128)}, u32[]{:S(2)}, u32[]{:S(2)}) collective-permute-start(f32[16,16,16]{1,0,2:T(8,128)S(1)} %get-tuple-element.29), channel_id=1, source_target_pairs={{1,0},{2,1},{3,2},{4,3},{5,4},{6,5},{7,6},{8,7},{9,8},{10,9},{11,1... | collective-permute-start | bytes 49160 | tf_op jit(solution)/shard_map/ppermute | solution.py:19
  625.5 9.8 %collective-permute-start.25 = (f32[16,16,16]{2,1,0:T(8,128)S(1)}, f32[16,16,16]{2,1,0:T(8,128)S(1)}, u32[]{:S(2)}, u32[]{:S(2)}) collective-permute-start(f32[16,16,16]{2,1,0:T(8,128)S(1)} %get-tuple-element.49), channel_id=1, source_target_pairs={{1,0},{2,1},{3,2},{4,3},{5,4},{6,5},{7,6},{8,7},{9,8},{10,9},{11,1... | collective-permute-start | bytes 49160 | tf_op jit(solution)/shard_map/ppermute | solution.py:19
  637.6 3.1 gather_fusion.16
  640.6 3.9 select_bitcast_fusion.1
  644.6 3.0 copy.472
  654.0 40.1 %scatter_fusion.10 = f32[16,16,160]{1,0,2:T(8,128)S(1)} fusion(f32[16,16,160]{1,0,2:T(8,128)S(1)} %broadcast.159.clone.4, s32[512]{0:T(512)S(1)} %fusion.27, f32[512,16,16]{2,1,0:T(8,128)} %bitcast.163), kind=kCustom, calls=%fused_computation.30 | custom fusion | flops 131072 | bytes 1574912 | tf_op jit(solution)/shard_map/scatter-add | solution.py:40
  697.8 10.0 %collective-permute-start.27 = (f32[16,16,16]{1,0,2:T(8,128)S(1)}, f32[16,16,16]{1,0,2:T(8,128)}, u32[]{:S(2)}, u32[]{:S(2)}) collective-permute-start(f32[16,16,16]{1,0,2:T(8,128)S(1)} %get-tuple-element.27), channel_id=1, source_target_pairs={{1,0},{2,1},{3,2},{4,3},{5,4},{6,5},{7,6},{8,7},{9,8},{10,9},{11,1... | collective-permute-start | bytes 49160 | tf_op jit(solution)/shard_map/ppermute | solution.py:19
  717.9 9.8 %collective-permute-start.29 = (f32[16,16,16]{2,1,0:T(8,128)S(1)}, f32[16,16,16]{2,1,0:T(8,128)S(1)}, u32[]{:S(2)}, u32[]{:S(2)}) collective-permute-start(f32[16,16,16]{2,1,0:T(8,128)S(1)} %get-tuple-element.47), channel_id=1, source_target_pairs={{1,0},{2,1},{3,2},{4,3},{5,4},{6,5},{7,6},{8,7},{9,8},{10,9},{11,1... | collective-permute-start | bytes 49160 | tf_op jit(solution)/shard_map/ppermute | solution.py:19
  730.5 3.1 gather_fusion.17
  733.6 3.9 select_bitcast_fusion
  737.5 3.1 copy.481
  745.8 40.1 %scatter_fusion.12 = f32[16,16,160]{1,0,2:T(8,128)S(1)} fusion(f32[16,16,160]{1,0,2:T(8,128)S(1)} %broadcast.159, s32[512]{0:T(512)S(1)} %fusion.27, f32[512,16,16]{2,1,0:T(8,128)} %bitcast.157), kind=kCustom, calls=%fused_computation.32 | custom fusion | flops 131072 | bytes 1574912 | tf_op jit(solution)/shard_map/scatter-add | solution.py:40
  788.6 9.5 %collective-permute-start.31 = (f32[16,16,16]{1,0,2:T(8,128)S(1)}, f32[16,16,16]{1,0,2:T(8,128)S(1)}, u32[]{:S(2)}, u32[]{:S(2)}) collective-permute-start(f32[16,16,16]{1,0,2:T(8,128)S(1)} %get-tuple-element.25), channel_id=1, source_target_pairs={{1,0},{2,1},{3,2},{4,3},{5,4},{6,5},{7,6},{8,7},{9,8},{10,9},{11,1... | collective-permute-start | bytes 49160 | tf_op jit(solution)/shard_map/ppermute | solution.py:19
  801.7 112.5 %all-reduce = (f32[48,48]{1,0:T(8,128)}, f32[48,48]{1,0:T(8,128)}) all-reduce(f32[48,48]{1,0:T(8,128)S(1)} %fusion.2, f32[48,48]{1,0:T(8,128)} %fusion.1), channel_id=1, replica_groups=mesh['dom'=512] {'dom'}, use_global_device_ids=true, to_apply=%region_50.52 | all-reduce | flops 4608 | bytes 36864 | tf_op jit(solution)/shard_map/psum | solution.py:144
  (286 shorter events, 182.6 us)
Async XLA Ops:
  0.6 22.3 %copy-start = (f32[4,16,16,128]{3,2,1,0:T(8,128)S(1)}, f32[4,16,16,128]{3,2,1,0:T(8,128)}, u32[]{:S(2)}) copy-start(f32[4,16,16,128]{3,2,1,0:T(8,128)} %param.14) | copy-start | bytes 1572868
  0.6 22.3 %copy-start.1 = (f32[4,16,16,128]{3,2,1,0:T(8,128)S(1)}, f32[4,16,16,128]{3,2,1,0:T(8,128)}, u32[]{:S(2)}) copy-start(f32[4,16,16,128]{3,2,1,0:T(8,128)} %param.15) | copy-start | bytes 1572868
  0.7 25.3 %copy-start.13 = (s32[128]{0:T(128)S(1)}, s32[128]{0:T(128)}, u32[]{:S(2)}) copy-start(s32[128]{0:T(128)} %param.21) | copy-start | bytes 1540
  0.7 25.4 %copy-start.8 = (f32[16,128]{1,0:T(8,128)S(1)}, f32[16,128]{1,0:T(8,128)}, u32[]{:S(2)}) copy-start(f32[16,128]{1,0:T(8,128)} %param.16) | copy-start | bytes 24580
  3.9 23.3 %copy-start.5 = (f32[16,32,128]{2,1,0:T(8,128)}, f32[16,32,128]{2,1,0:T(8,128)S(1)}, u32[]{:S(2)}) copy-start(f32[16,32,128]{2,1,0:T(8,128)S(1)} %constant_dynamic-update-slice_fusion) | copy-start | bytes 786436
  5.1 22.1 %collective-permute-start = (f32[16,32,16]{1,0,2:T(8,128)S(1)}, f32[16,32,16]{1,0,2:T(8,128)S(1)}, u32[]{:S(2)}, u32[]{:S(2)}) collective-permute-start(f32[16,32,16]{1,0,2:T(8,128)S(1)} %get-tuple-element.42), channel_id=1, source_target_pairs={{0,1},{1,2},{2,3},{3,4},{4,5},{5,6},{6,7},{7,8},{8,9},{9,10},{10,1... | collective-permute-start | bytes 98312 | tf_op jit(solution)/shard_map/ppermute | solution.py:18
  9.7 18.2 %collective-permute-start.1 = (f32[16,32,16]{1,0,2:T(8,128)S(1)}, f32[16,32,16]{1,0,2:T(8,128)}, u32[]{:S(2)}, u32[]{:S(2)}) collective-permute-start(f32[16,32,16]{1,0,2:T(8,128)S(1)} %get-tuple-element.43), channel_id=1, source_target_pairs={{1,0},{2,1},{3,2},{4,3},{5,4},{6,5},{7,6},{8,7},{9,8},{10,9},{11,1... | collective-permute-start | bytes 98312 | tf_op jit(solution)/shard_map/ppermute | solution.py:19
  27.2 0.7 copy-start.10
  35.9 4.8 copy-start.2
  90.2 14.1 %collective-permute-start.2 = (f32[16,33,16]{1,0,2:T(8,128)}, f32[16,33,16]{1,0,2:T(8,128)}, u32[]{:S(2)}, u32[]{:S(2)}) collective-permute-start(f32[16,33,16]{1,0,2:T(8,128)} %get-tuple-element.39), channel_id=1, source_target_pairs={{0,1},{1,2},{2,3},{3,4},{4,5},{5,6},{6,7},{7,8},{8,9},{9,10},{10,1... | collective-permute-start | bytes 101384 | tf_op jit(solution)/shard_map/ppermute | solution.py:18
  92.1 13.1 %collective-permute-start.3 = (f32[16,33,16]{1,0,2:T(8,128)}, f32[16,33,16]{1,0,2:T(8,128)}, u32[]{:S(2)}, u32[]{:S(2)}) collective-permute-start(f32[16,33,16]{1,0,2:T(8,128)} %get-tuple-element.38), channel_id=1, source_target_pairs={{1,0},{2,1},{3,2},{4,3},{5,4},{6,5},{7,6},{8,7},{9,8},{10,9},{11,1... | collective-permute-start | bytes 101384 | tf_op jit(solution)/shard_map/ppermute | solution.py:19
  104.2 6.3 copy-start.4
  229.5 6.4 collective-permute-start.4
  231.5 6.3 collective-permute-start.5
  245.5 3.9 copy-start.7
  295.2 12.3 %collective-permute-start.6 = (f32[16,16,16]{1,0,2:T(8,128)S(1)}, f32[16,16,16]{1,0,2:T(8,128)S(1)}, u32[]{:S(2)}, u32[]{:S(2)}) collective-permute-start(f32[16,16,16]{1,0,2:T(8,128)S(1)} %get-tuple-element.34), channel_id=1, source_target_pairs={{0,1},{1,2},{2,3},{3,4},{4,5},{5,6},{6,7},{7,8},{8,9},{9,10},{10,1... | collective-permute-start | bytes 49160 | tf_op jit(solution)/shard_map/ppermute | solution.py:18
  297.1 10.3 %collective-permute-start.7 = (f32[16,16,16]{1,0,2:T(8,128)S(1)}, f32[16,16,16]{1,0,2:T(8,128)S(1)}, u32[]{:S(2)}, u32[]{:S(2)}) collective-permute-start(f32[16,16,16]{1,0,2:T(8,128)S(1)} %get-tuple-element.35), channel_id=1, source_target_pairs={{1,0},{2,1},{3,2},{4,3},{5,4},{6,5},{7,6},{8,7},{9,8},{10,9},{11,1... | collective-permute-start | bytes 49160 | tf_op jit(solution)/shard_map/ppermute | solution.py:19
  310.9 13.2 %collective-permute-start.8 = (f32[16,16,16]{2,1,0:T(8,128)S(1)}, f32[16,16,16]{2,1,0:T(8,128)S(1)}, u32[]{:S(2)}, u32[]{:S(2)}) collective-permute-start(f32[16,16,16]{2,1,0:T(8,128)S(1)} %get-tuple-element.54), channel_id=1, source_target_pairs={{0,1},{1,2},{2,3},{3,4},{4,5},{5,6},{6,7},{7,8},{8,9},{9,10},{10,1... | collective-permute-start | bytes 49160 | tf_op jit(solution)/shard_map/ppermute | solution.py:18
  312.9 11.3 %collective-permute-start.9 = (f32[16,16,16]{2,1,0:T(8,128)S(1)}, f32[16,16,16]{2,1,0:T(8,128)S(1)}, u32[]{:S(2)}, u32[]{:S(2)}) collective-permute-start(f32[16,16,16]{2,1,0:T(8,128)S(1)} %get-tuple-element.55), channel_id=1, source_target_pairs={{1,0},{2,1},{3,2},{4,3},{5,4},{6,5},{7,6},{8,7},{9,8},{10,9},{11,1... | collective-permute-start | bytes 49160 | tf_op jit(solution)/shard_map/ppermute | solution.py:19
  383.2 14.0 %collective-permute-start.10 = (f32[16,16,16]{1,0,2:T(8,128)}, f32[16,16,16]{1,0,2:T(8,128)S(1)}, u32[]{:S(2)}, u32[]{:S(2)}) collective-permute-start(f32[16,16,16]{1,0,2:T(8,128)} %get-tuple-element.32), channel_id=1, source_target_pairs={{0,1},{1,2},{2,3},{3,4},{4,5},{5,6},{6,7},{7,8},{8,9},{9,10},{10,1... | collective-permute-start | bytes 49160 | tf_op jit(solution)/shard_map/ppermute | solution.py:18
  385.1 12.1 %collective-permute-start.11 = (f32[16,16,16]{1,0,2:T(8,128)S(1)}, f32[16,16,16]{1,0,2:T(8,128)}, u32[]{:S(2)}, u32[]{:S(2)}) collective-permute-start(f32[16,16,16]{1,0,2:T(8,128)S(1)} %get-tuple-element.33), channel_id=1, source_target_pairs={{1,0},{2,1},{3,2},{4,3},{5,4},{6,5},{7,6},{8,7},{9,8},{10,9},{11,1... | collective-permute-start | bytes 49160 | tf_op jit(solution)/shard_map/ppermute | solution.py:19
  401.7 11.5 %collective-permute-start.12 = (f32[16,17,16]{2,1,0:T(8,128)S(1)}, f32[16,17,16]{2,1,0:T(8,128)S(1)}, u32[]{:S(2)}, u32[]{:S(2)}) collective-permute-start(f32[16,17,16]{2,1,0:T(8,128)S(1)} %get-tuple-element.44), channel_id=1, source_target_pairs={{0,1},{1,2},{2,3},{3,4},{4,5},{5,6},{6,7},{7,8},{8,9},{9,10},{10,1... | collective-permute-start | bytes 52232 | tf_op jit(solution)/shard_map/ppermute | solution.py:18
  403.7 10.6 %collective-permute-start.13 = (f32[16,17,16]{2,1,0:T(8,128)S(1)}, f32[16,17,16]{2,1,0:T(8,128)S(1)}, u32[]{:S(2)}, u32[]{:S(2)}) collective-permute-start(f32[16,17,16]{2,1,0:T(8,128)S(1)} %get-tuple-element.45), channel_id=1, source_target_pairs={{1,0},{2,1},{3,2},{4,3},{5,4},{6,5},{7,6},{8,7},{9,8},{10,9},{11,1... | collective-permute-start | bytes 52232 | tf_op jit(solution)/shard_map/ppermute | solution.py:19
  419.9 15.3 %collective-permute-start.14 = (f32[16,16,16]{2,1,0:T(8,128)S(1)}, f32[16,16,16]{2,1,0:T(8,128)S(1)}, u32[]{:S(2)}, u32[]{:S(2)}) collective-permute-start(f32[16,16,16]{2,1,0:T(8,128)S(1)} %get-tuple-element.52), channel_id=1, source_target_pairs={{0,1},{1,2},{2,3},{3,4},{4,5},{5,6},{6,7},{7,8},{8,9},{9,10},{10,1... | collective-permute-start | bytes 49160 | tf_op jit(solution)/shard_map/ppermute | solution.py:18
  421.8 13.4 %collective-permute-start.15 = (f32[16,16,16]{2,1,0:T(8,128)S(1)}, f32[16,16,16]{2,1,0:T(8,128)S(1)}, u32[]{:S(2)}, u32[]{:S(2)}) collective-permute-start(f32[16,16,16]{2,1,0:T(8,128)S(1)} %get-tuple-element.53), channel_id=1, source_target_pairs={{1,0},{2,1},{3,2},{4,3},{5,4},{6,5},{7,6},{8,7},{9,8},{10,9},{11,1... | collective-permute-start | bytes 49160 | tf_op jit(solution)/shard_map/ppermute | solution.py:19
  495.9 13.8 %collective-permute-start.16 = (f32[16,16,16]{1,0,2:T(8,128)}, f32[16,16,16]{1,0,2:T(8,128)S(1)}, u32[]{:S(2)}, u32[]{:S(2)}) collective-permute-start(f32[16,16,16]{1,0,2:T(8,128)} %get-tuple-element.30), channel_id=1, source_target_pairs={{0,1},{1,2},{2,3},{3,4},{4,5},{5,6},{6,7},{7,8},{8,9},{9,10},{10,1... | collective-permute-start | bytes 49160 | tf_op jit(solution)/shard_map/ppermute | solution.py:18
  497.8 12.6 %collective-permute-start.17 = (f32[16,16,16]{1,0,2:T(8,128)}, f32[16,16,16]{1,0,2:T(8,128)}, u32[]{:S(2)}, u32[]{:S(2)}) collective-permute-start(f32[16,16,16]{1,0,2:T(8,128)} %get-tuple-element.31), channel_id=1, source_target_pairs={{1,0},{2,1},{3,2},{4,3},{5,4},{6,5},{7,6},{8,7},{9,8},{10,9},{11,1... | collective-permute-start | bytes 49160 | tf_op jit(solution)/shard_map/ppermute | solution.py:19
  509.8 0.7 copy-start.12
  514.4 13.8 %collective-permute-start.18 = (f32[16,16,16]{1,0,2:T(8,128)}, f32[16,16,16]{1,0,2:T(8,128)S(1)}, u32[]{:S(2)}, u32[]{:S(2)}) collective-permute-start(f32[16,16,16]{1,0,2:T(8,128)} %get-tuple-element.40), channel_id=1, source_target_pairs={{0,1},{1,2},{2,3},{3,4},{4,5},{5,6},{6,7},{7,8},{8,9},{9,10},{10,1... | collective-permute-start | bytes 49160 | tf_op jit(solution)/shard_map/ppermute | solution.py:18
  516.3 11.9 %collective-permute-start.19 = (f32[16,16,16]{1,0,2:T(8,128)}, f32[16,16,16]{1,0,2:T(8,128)S(1)}, u32[]{:S(2)}, u32[]{:S(2)}) collective-permute-start(f32[16,16,16]{1,0,2:T(8,128)} %get-tuple-element.41), channel_id=1, source_target_pairs={{1,0},{2,1},{3,2},{4,3},{5,4},{6,5},{7,6},{8,7},{9,8},{10,9},{11,1... | collective-permute-start | bytes 49160 | tf_op jit(solution)/shard_map/ppermute | solution.py:19
  533.1 13.1 %collective-permute-start.20 = (f32[16,16,16]{2,1,0:T(8,128)S(1)}, f32[16,16,16]{2,1,0:T(8,128)S(1)}, u32[]{:S(2)}, u32[]{:S(2)}) collective-permute-start(f32[16,16,16]{2,1,0:T(8,128)S(1)} %get-tuple-element.50), channel_id=1, source_target_pairs={{0,1},{1,2},{2,3},{3,4},{4,5},{5,6},{6,7},{7,8},{8,9},{9,10},{10,1... | collective-permute-start | bytes 49160 | tf_op jit(solution)/shard_map/ppermute | solution.py:18
  535.1 11.1 %collective-permute-start.21 = (f32[16,16,16]{2,1,0:T(8,128)S(1)}, f32[16,16,16]{2,1,0:T(8,128)S(1)}, u32[]{:S(2)}, u32[]{:S(2)}) collective-permute-start(f32[16,16,16]{2,1,0:T(8,128)S(1)} %get-tuple-element.51), channel_id=1, source_target_pairs={{1,0},{2,1},{3,2},{4,3},{5,4},{6,5},{7,6},{8,7},{9,8},{10,9},{11,1... | collective-permute-start | bytes 49160 | tf_op jit(solution)/shard_map/ppermute | solution.py:19
  605.2 13.9 %collective-permute-start.22 = (f32[16,16,16]{1,0,2:T(8,128)}, f32[16,16,16]{1,0,2:T(8,128)S(1)}, u32[]{:S(2)}, u32[]{:S(2)}) collective-permute-start(f32[16,16,16]{1,0,2:T(8,128)} %get-tuple-element.28), channel_id=1, source_target_pairs={{0,1},{1,2},{2,3},{3,4},{4,5},{5,6},{6,7},{7,8},{8,9},{9,10},{10,1... | collective-permute-start | bytes 49160 | tf_op jit(solution)/shard_map/ppermute | solution.py:18
  607.1 12.0 %collective-permute-start.23 = (f32[16,16,16]{1,0,2:T(8,128)S(1)}, f32[16,16,16]{1,0,2:T(8,128)}, u32[]{:S(2)}, u32[]{:S(2)}) collective-permute-start(f32[16,16,16]{1,0,2:T(8,128)S(1)} %get-tuple-element.29), channel_id=1, source_target_pairs={{1,0},{2,1},{3,2},{4,3},{5,4},{6,5},{7,6},{8,7},{9,8},{10,9},{11,1... | collective-permute-start | bytes 49160 | tf_op jit(solution)/shard_map/ppermute | solution.py:19
  623.5 13.3 %collective-permute-start.24 = (f32[16,16,16]{2,1,0:T(8,128)S(1)}, f32[16,16,16]{2,1,0:T(8,128)S(1)}, u32[]{:S(2)}, u32[]{:S(2)}) collective-permute-start(f32[16,16,16]{2,1,0:T(8,128)S(1)} %get-tuple-element.48), channel_id=1, source_target_pairs={{0,1},{1,2},{2,3},{3,4},{4,5},{5,6},{6,7},{7,8},{8,9},{9,10},{10,1... | collective-permute-start | bytes 49160 | tf_op jit(solution)/shard_map/ppermute | solution.py:18
  625.5 11.4 %collective-permute-start.25 = (f32[16,16,16]{2,1,0:T(8,128)S(1)}, f32[16,16,16]{2,1,0:T(8,128)S(1)}, u32[]{:S(2)}, u32[]{:S(2)}) collective-permute-start(f32[16,16,16]{2,1,0:T(8,128)S(1)} %get-tuple-element.49), channel_id=1, source_target_pairs={{1,0},{2,1},{3,2},{4,3},{5,4},{6,5},{7,6},{8,7},{9,8},{10,9},{11,1... | collective-permute-start | bytes 49160 | tf_op jit(solution)/shard_map/ppermute | solution.py:19
  695.9 14.0 %collective-permute-start.26 = (f32[16,16,16]{1,0,2:T(8,128)}, f32[16,16,16]{1,0,2:T(8,128)S(1)}, u32[]{:S(2)}, u32[]{:S(2)}) collective-permute-start(f32[16,16,16]{1,0,2:T(8,128)} %get-tuple-element.26), channel_id=1, source_target_pairs={{0,1},{1,2},{2,3},{3,4},{4,5},{5,6},{6,7},{7,8},{8,9},{9,10},{10,1... | collective-permute-start | bytes 49160 | tf_op jit(solution)/shard_map/ppermute | solution.py:18
  697.8 12.1 %collective-permute-start.27 = (f32[16,16,16]{1,0,2:T(8,128)S(1)}, f32[16,16,16]{1,0,2:T(8,128)}, u32[]{:S(2)}, u32[]{:S(2)}) collective-permute-start(f32[16,16,16]{1,0,2:T(8,128)S(1)} %get-tuple-element.27), channel_id=1, source_target_pairs={{1,0},{2,1},{3,2},{4,3},{5,4},{6,5},{7,6},{8,7},{9,8},{10,9},{11,1... | collective-permute-start | bytes 49160 | tf_op jit(solution)/shard_map/ppermute | solution.py:19
  713.0 88.2 %copy-start.3 = (f32[16,16,128]{2,1,0:T(8,128)}, f32[16,16,128]{2,1,0:T(8,128)S(1)}, u32[]{:S(2)}) copy-start(f32[16,16,128]{2,1,0:T(8,128)S(1)} %multiply_add_fusion.2) | copy-start | bytes 393220
  715.9 13.8 %collective-permute-start.28 = (f32[16,16,16]{2,1,0:T(8,128)S(1)}, f32[16,16,16]{2,1,0:T(8,128)S(1)}, u32[]{:S(2)}, u32[]{:S(2)}) collective-permute-start(f32[16,16,16]{2,1,0:T(8,128)S(1)} %get-tuple-element.46), channel_id=1, source_target_pairs={{0,1},{1,2},{2,3},{3,4},{4,5},{5,6},{6,7},{7,8},{8,9},{9,10},{10,1... | collective-permute-start | bytes 49160 | tf_op jit(solution)/shard_map/ppermute | solution.py:18
  717.9 11.9 %collective-permute-start.29 = (f32[16,16,16]{2,1,0:T(8,128)S(1)}, f32[16,16,16]{2,1,0:T(8,128)S(1)}, u32[]{:S(2)}, u32[]{:S(2)}) collective-permute-start(f32[16,16,16]{2,1,0:T(8,128)S(1)} %get-tuple-element.47), channel_id=1, source_target_pairs={{1,0},{2,1},{3,2},{4,3},{5,4},{6,5},{7,6},{8,7},{9,8},{10,9},{11,1... | collective-permute-start | bytes 49160 | tf_op jit(solution)/shard_map/ppermute | solution.py:19
  737.5 3.9 copy-start.6
  786.0 15.3 %copy-start.9 = (f32[16,16,128]{2,1,0:T(8,128)S(1)}, f32[16,16,128]{2,1,0:T(8,128)}, u32[]{:S(2)}) copy-start(f32[16,16,128]{2,1,0:T(8,128)} %copy.521) | copy-start | bytes 393220
  786.0 15.3 %copy-start.11 = (f32[16,16,128]{2,1,0:T(8,128)S(1)}, f32[16,16,128]{2,1,0:T(8,128)}, u32[]{:S(2)}) copy-start(f32[16,16,128]{2,1,0:T(8,128)} %param.13) | copy-start | bytes 393220
  786.7 12.4 %collective-permute-start.30 = (f32[16,16,16]{1,0,2:T(8,128)}, f32[16,16,16]{1,0,2:T(8,128)S(1)}, u32[]{:S(2)}, u32[]{:S(2)}) collective-permute-start(f32[16,16,16]{1,0,2:T(8,128)} %get-tuple-element.24), channel_id=1, source_target_pairs={{0,1},{1,2},{2,3},{3,4},{4,5},{5,6},{6,7},{7,8},{8,9},{9,10},{10,1... | collective-permute-start | bytes 49160 | tf_op jit(solution)/shard_map/ppermute | solution.py:18
  788.6 10.5 %collective-permute-start.31 = (f32[16,16,16]{1,0,2:T(8,128)S(1)}, f32[16,16,16]{1,0,2:T(8,128)S(1)}, u32[]{:S(2)}, u32[]{:S(2)}) collective-permute-start(f32[16,16,16]{1,0,2:T(8,128)S(1)} %get-tuple-element.25), channel_id=1, source_target_pairs={{1,0},{2,1},{3,2},{4,3},{5,4},{6,5},{7,6},{8,7},{9,8},{10,9},{11,1... | collective-permute-start | bytes 49160 | tf_op jit(solution)/shard_map/ppermute | solution.py:19
where the time goes:
time: 924 us; the launch traced here: 915 us
  other arithmetic  380 us (41%)
  blocking collectives  223 us (24%)
  starting transfers between devices  179 us (19%)
  local copies, waits for them, and re-layouts  122 us (13%)
    scatter-add x7, other arithmetic, edge_terms(): gathered = jnp.zeros(extended.shape, jnp.float32).at[:, :, block_cols].ad...  281 us
    ppermute x16, starting transfers between devices, extended_2(): after = lax.ppermute(first, axis, down)  146 us
    psum x1, blocking collectives, shards(): lax.psum((gram_block(basis, images, norm_scale), gram_block(basis, basis,...  113 us
    psum x1, blocking collectives, shards(): lax.psum((gram_block(x_block, x_block, norm_scale), gram_block(x_block, i...  111 us
    ppermute x16, starting transfers between devices, extended_2(): before = lax.ppermute(last, axis, up)  33.3 us
    transpose x6, other arithmetic, edge_terms(): remote = jnp.moveaxis(jnp.take(extended, block_cols, axis=2), 2, 0)  23.5 us
    gather x7, local copies, waits for them, and re-layouts, edge_terms(): remote = jnp.moveaxis(jnp.take(extended, block_cols, axis=2), 2, 0)  21.4 us
    neg x7, local copies, waits for them, and re-layouts, edge_terms(): -jnp.moveaxis(far_part, 0, 2)  19.8 us
  transfers between devices with their start and end apart: 32, of which 2 were waited for; matrix products, arithmetic and copies ran while one was open for 4% of the time, Pallas kernels for 0%

commit v1 on v0

v1 whole, which is shorter than its diff:
```python
import functools

import jax
import jax.numpy as jnp
from jax import lax
from jax.experimental import pallas as pl
from jax.experimental.pallas import tpu as pltpu
from jax.sharding import PartitionSpec as P

MESH = pl.DeviceIdType.MESH
f32 = jnp.float32
bf16 = jnp.bfloat16
S = 16
C = 16
K = 4
N = 128
H = 32
T = 2
LAST = 8


def iota(shape, dim):
    return lax.broadcasted_iota(jnp.int32, shape, dim)


def one_hot(mask):
    return jnp.where(mask, 1.0, 0.0).astype(f32)


def split(value):
    terms = []
    for t in range(T):
        term = value.astype(bf16)
        terms.append(term)
        if t + 1 < T:
            value = value - term.astype(f32)
    return terms


def dot_nn(a, b):
    return jnp.dot(a, b, preferred_element_type=f32)


def dot_nt(a, b):
    return lax.dot_general(a, b, (((1,), (1,)), ((), ())), preferred_element_type=f32)


def dot_tn(a, b):
    return lax.dot_general(a, b, (((0,), (0,)), ((), ())), preferred_element_type=f32)


class Groups:
    def __init__(self, me, dims):
        self.me, self.dims = me, dims
        self.size = 1
        for _, g in dims:
            self.size *= g
        self.pos = 0
        self.base = me
        for s, g in dims:
            p = lax.rem(lax.div(me, s), g)
            self.pos = self.pos * g + p
            self.base = self.base - p * s

    def device(self, pos):
        d = self.base
        for s, g in reversed(self.dims):
            d = d + lax.rem(pos, g) * s
            pos = lax.div(pos, g)
        return d

    def peer(self, t):
        return lax.rem(self.pos + t, self.size)


def kernel(
    n_dom, ar_dims,
    x_ref, p_ref, own_ref, oth_ref, mass_ref, cols_ref, deg_ref, send_ref, pair_ref, part_ref,
    out_ref, ga_ref, gb_ref,
    B, D, hd, hdc, diag, v, y, e, acc, vv, w_ref, qb, gram1, gram2,
    vcat, wcat, rr, Gl, GH, GHs, ST, Pn, Pr, PPn, Ql, Qh,
    sndh, rcvh, sndc, rcvc, sndd, rcvd, ar_bufs,
    hs, hr, cs, cr, ds, dr, ar_ss, ar_rs,
):
    me = lax.axis_index("dom")
    lower = lax.rem(me + n_dom - 1, n_dom)
    upper = lax.rem(me + 1, n_dom)
    groups = [[Groups(me, dims) for dims in stages] for stages in ar_dims]
    bar_groups = groups[1]

    barrier = pltpu.get_barrier_semaphore()
    for d in (lower, upper):
        pl.semaphore_signal(barrier, inc=1, device_id=(d,), device_id_type=MESH)
    n_bar = 2
    for g in bar_groups:
        n_bar += g.size - 1

        def greet(t, _, g=g):
            pl.semaphore_signal(barrier, inc=1, device_id=(g.device(g.peer(t)),), device_id_type=MESH)
            return 0

        lax.fori_loop(1, g.size, greet, 0)

    def pair_copies(snd, rcv, ss, rs, idx):
        out = []
        for side, (src, dst, dev) in enumerate(((0, 16, lower), (16, 0, upper))):
            out.append(
                pltpu.make_async_remote_copy(
                    snd.at[idx + (pl.ds(src, 16),)],
                    rcv.at[idx + (pl.ds(dst, 16),)],
                    ss.at[idx + (side,)],
                    rs.at[idx + (side,)],
                    device_id=(dev,),
                    device_id_type=MESH,
                )
            )
        return out

    def start(*args):
        for c in pair_copies(*args):
            c.start()

    def wait_recv(*args):
        for c in pair_copies(*args):
            c.wait_recv()

    def wait_send(*args):
        for c in pair_copies(*args):
            c.wait_send()

    def ar_copy(slot, stage, t, receive):
        g = groups[slot][stage]
        peer = g.peer(t)
        buf = ar_bufs[slot][stage]
        at = peer if receive else g.pos
        return pltpu.make_async_remote_copy(
            buf.at[g.pos],
            buf.at[at],
            ar_ss[slot][stage].at[peer],
            ar_rs[slot][stage].at[at],
            device_id=(g.device(peer),),
            device_id_type=MESH,
        )

    def ar_start(slot, stage, value):
        g = groups[slot][stage]
        ar_bufs[slot][stage][g.pos] = value

        def go(t, _):
            ar_copy(slot, stage, t, False).start()
            return 0

        lax.fori_loop(1, g.size, go, 0)

    def ar_finish(slot, stage):
        g = groups[slot][stage]

        def go(t, _):
            ar_copy(slot, stage, t, True).wait_recv()
            return 0

        lax.fori_loop(1, g.size, go, 0)
        buf = ar_bufs[slot][stage]
        total = buf[0]
        for j in range(1, g.size):
            total = total + buf[j]
        return total

    def ar_drain(slot, stage):
        g = groups[slot][stage]

        def go(t, _):
            ar_copy(slot, stage, t, False).wait_send()
            return 0

        lax.fori_loop(1, g.size, go, 0)

    for k in range(K):
        at_k = pl.ds(k * N, N)
        hot = one_hot(iota((N, N), 0) == cols_ref[k : k + 1, :])
        hot_t = hot.T.astype(bf16)
        halo = one_hot(iota((H, N), 0) + N == cols_ref[k : k + 1, :]).astype(bf16)
        hot = hot.astype(bf16)
        for t in range(T):
            Gl[pl.ds(t * N, N), at_k] = hot
            ST[pl.ds((t * K + k) * N, N), :] = hot_t
            GH[:, pl.ds((t * K + k) * N, N)] = halo
            GHs[pl.ds(t * H, H), at_k] = halo
    hot = one_hot(iota((N, N), 0) == part_ref[...]).astype(bf16)
    halo = one_hot(iota((H, N), 0) + N == part_ref[...]).astype(bf16)
    for t in range(T):
        Ql[pl.ds(t * N, N), :] = hot
        Qh[pl.ds(t * H, H), :] = halo

    def column(ref):
        square = jnp.where(iota((H, H), 0) == iota((H, H), 1), ref[...].astype(f32), 0.0)
        return jnp.sum(square, axis=1, keepdims=True)

    lanes = iota((H, N), 1).astype(f32)
    sel = one_hot(lanes == column(send_ref)).astype(bf16)
    psel = one_hot(lanes == column(pair_ref)).astype(bf16)
    for t in range(T):
        Pn[:, pl.ds(t * N, N)] = sel
        Pr[pl.ds(t * H, H), :] = sel
        PPn[:, pl.ds(t * N, N)] = psel

    def bcast_rows(ref, idx, r):
        return ref[idx + (slice(r, r + 1), slice(None))]

    def store_split_w(k, b, value):
        for t, term in enumerate(split(value)):
            wcat[pl.ds(b * C, C), pl.ds(pl.multiple_of(t * K * N + k * N, N), N)] = term

    def store_split_v(ref):
        for b in range(S):
            for t, term in enumerate(split(ref[b])):
                vcat[pl.ds(b * C, C), pl.ds(t * N, N)] = term

    def scatter_halo():
        return dot_nt(GH[...], wcat[...])

    def scatter_local():
        return dot_nn(wcat[...], ST[...])

    def from_halo(rows, matrix):
        return dot_tn(jnp.concatenate(split(rows), axis=0), matrix[...])

    def reverse(ref):
        def body(k, _):
            for half in range(2):
                total = [jnp.zeros((C, N), f32)] * 8
                for a in range(S):
                    value = ref[a]
                    for j in range(8):
                        total[j] = total[j] + bcast_rows(B, (k, a), half * 8 + j) * value
                for j in range(8):
                    store_split_w(k, half * 8 + j, total[j])
            return 0

        lax.fori_loop(0, K, body, 0)

    def far(src):
        def body(k, total):
            total = list(total)
            for b in range(S):
                value = src[k, b]
                for a in range(S):
                    total[a] = total[a] + bcast_rows(B, (k, a), b) * value
            return tuple(total)

        return lax.fori_loop(0, K, body, tuple(jnp.zeros((C, N), f32) for _ in range(S)))

    def own(ref, factor=None):
        total = [jnp.zeros((C, N), f32)] * S
        for b in range(S):
            value = ref[b]
            for a in range(S):
                total[a] = total[a] + bcast_rows(D, (a,), b) * value
        return total

    def gather_local(dst):
        rows = dot_nn(vcat[...], Gl[...])
        for k in range(K):
            dst[k] = rows[:, k * N : (k + 1) * N].reshape(S, C, N)

    def gather_halo(rows, dst):
        got = from_halo(rows, GHs)
        for k in range(K):
            dst[k] = dst[k] + got[:, k * N : (k + 1) * N].reshape(S, C, N)

    def a_start(i, ch, with_own=True):
        src = v.at[ch]
        store_split_v(src)
        sndh[i, ch] = dot_nt(Pn[...], vcat[...])
        start(sndh, rcvh, hs, hr, (i, ch))
        reverse(src)
        sndc[i, ch] = scatter_halo()
        start(sndc, rcvc, cs, cr, (i, ch))
        back = scatter_local().reshape(S, C, N)
        gather_local(vv.at[ch])
        if with_own:
            total = own(src)
            for a in range(S):
                acc[ch, a] = total[a] - back[a]
        else:
            acc[ch] = -back

    def a_finish(i, ch):
        wait_recv(sndh, rcvh, hs, hr, (i, ch))
        gather_halo(rcvh[i, ch], vv.at[ch])
        total = far(vv.at[ch])
        wait_recv(sndc, rcvc, cs, cr, (i, ch))
        got = from_halo(rcvc[i, ch], Pr).reshape(S, C, N)
        for a in range(S):
            y[ch, a] = y[ch, a] - acc[ch, a] + total[a] + got[a]

    def q_start(i, ch):
        store_split_v(y.at[ch])
        sndh[i, ch] = dot_nt(PPn[...], vcat[...])
        start(sndh, rcvh, hs, hr, (i, ch))
        acc[ch] = y[ch] + dot_nn(vcat[...], Ql[...]).reshape(S, C, N)

    def q_finish(i, ch):
        wait_recv(sndh, rcvh, hs, hr, (i, ch))
        got = from_halo(rcvh[i, ch], Qh).reshape(S, C, N)
        for b in range(S):
            value = (acc[ch, b] + got[b]) * hdc[b : b + 1, :]
            v[ch, b] = value
            e[ch, b] = e[ch, b] + value

    def smooth(ch):
        for b in range(S):
            value = y[ch, b] * hd[b : b + 1, :]
            v[ch, b] = value
            e[ch, b] = e[ch, b] + value

    def rr_store(row, ref, sign=1.0):
        for b in range(S):
            for t, term in enumerate(split(sign * ref[b])):
                rr[pl.ds(t * 128 + row, C), pl.ds(b * N, N)] = term

    live = [jnp.where(deg_ref[...] > k, 1.0, 0.0).astype(f32) for k in range(K)]

    def outer(left, right, k):
        def body(s, total):
            value = right[k, s]
            return tuple(total[a] + left[k, s, a : a + 1, :] * value for a in range(S))

        return lax.fori_loop(0, S, body, tuple(jnp.zeros((S, N), f32) for _ in range(S)), unroll=4)

    rr[...] = jnp.zeros_like(rr)
    for k in range(K):
        for a, value in enumerate(outer(oth_ref, oth_ref, k)):
            store_split_w(k, a, value * live[k])
    sndc[LAST, 0] = scatter_halo()
    D[...] = scatter_local().reshape(S, S, N)
    for k in range(K):
        for a, value in enumerate(outer(own_ref, own_ref, k)):
            D[a] = D[a] + value * live[k]
        for a, value in enumerate(outer(own_ref, oth_ref, k)):
            B[k, a] = value * live[k]
    for b in range(S):
        D[b, b : b + 1, :] = D[b, b : b + 1, :] + mass_ref[b : b + 1, :]
    e[...] = jnp.zeros_like(e)
    y[...] = jnp.zeros_like(y)
    v[0] = p_ref[...]
    v[1] = x_ref[...]
    rr_store(0, x_ref)
    rr_store(16, p_ref)

    pl.semaphore_wait(barrier, n_bar)

    start(sndc, rcvc, cs, cr, (LAST, 0))
    a_start(0, 1, False)
    a_start(0, 0, False)

    wait_recv(sndc, rcvc, cs, cr, (LAST, 0))
    D[...] = D[...] + from_halo(rcvc[LAST, 0], Pr).reshape(S, S, N)
    for b in range(S):
        diag[b : b + 1, :] = D[b, b : b + 1, :]
    hd[...] = 0.5 / diag[...]
    dcat = jnp.concatenate(split(diag[...]), axis=1)
    sndd[...] = jnp.zeros_like(sndd)
    sndd[:, 0:S] = dot_nt(PPn[...], dcat)
    start(sndd, rcvd, ds, dr, ())
    for ch in (1, 0):
        total = own(v.at[ch])
        for a in range(S):
            acc[ch, a] = acc[ch, a] + total[a]

    def event(g, _):
        i = 1 + lax.div(g, 2)
        ch = 1 - lax.rem(g, 2)
        coarse_end = (i == 4) | (i == 6)
        coarse_start = (i == 3) | (i == 5)

        @pl.when(jnp.logical_not(coarse_end))
        def _():
            a_finish(i - 1, ch)

        @pl.when((i == 1) & (ch == 1))
        def _():
            rr_store(32, y.at[1], -1.0)

        @pl.when((i == 1) & (ch == 0))
        def _():
            rr_store(48, y.at[0], -1.0)
            y[0] = x_ref[...]

        @pl.when(coarse_end)
        def _():
            q_finish(i - 1, ch)

        @pl.when(jnp.logical_not(coarse_end | coarse_start))
        def _():
            smooth(ch)

        @pl.when(coarse_start)
        def _():
            q_start(i, ch)

        @pl.when(jnp.logical_not(coarse_start))
        def _():
            a_start(i, ch)

        late = ch == 0

        @pl.when(late & (i == 1))
        def _():
            left = jnp.concatenate([rr[0:32, :], rr[128:160, :]], axis=0)
            parts = dot_nt(left, rr[...])
            parts = parts[:, 0:128] + parts[:, 128:256]
            parts = (parts[0:32] + parts[32:64]) * (1.0 / (N * S * n_dom))
            rolled = pltpu.roll(parts[16:32], 64, 1)
            ar_start(0, 0, jnp.where(iota((C, 128), 1) < 64, parts[0:16], rolled))

        @pl.when(late & (i == 2))
        def _():
            wait_recv(sndd, rcvd, ds, dr, ())
            dcat = jnp.concatenate(split(diag[...]), axis=1)
            far_diag = from_halo(rcvd[...], Qh)[0:S]
            hdc[...] = 0.5 / (diag[...] + dot_nn(dcat, Ql[...]) + far_diag)

        stages = len(groups[0])
        for s in range(stages):

            @pl.when(late & (i == (2 + s if s + 1 < stages else 3 + s)))
            def _(s=s):
                total = ar_finish(0, s)
                if s + 1 < stages:
                    ar_start(0, s + 1, total)
                else:
                    gram1[...] = total
                    lane = iota((C, 128), 1)
                    work = jnp.where(lane < 16, total, jnp.where(lane < 32, pltpu.roll(total, 112, 1), 0.0))
                    for j in range(C):
                        col = jnp.sum(jnp.where(lane == j, work, 0.0), axis=1, keepdims=True)
                        row = work[j : j + 1, :] / col[j : j + 1, :]
                        unit = jnp.where(iota((C, 1), 0) == j, 1.0, 0.0)
                        work = work - (col - unit) * row
                    square = jnp.concatenate([work, jnp.zeros((128 - C, 128), f32)], axis=0).T
                    quot_t = square[16:32, :]
                    for j in range(C):
                        col = jnp.sum(jnp.where(lane == j, quot_t, 0.0), axis=1, keepdims=True)
                        qb[j] = jnp.broadcast_to(col, (C, 128))

        return 0

    lax.fori_loop(0, 2 * (LAST - 1), event, 0)

    def last_event(g, _):
        ch = g
        a_finish(LAST - 1, ch)
        for b in range(S):
            e[ch, b] = e[ch, b] + y[ch, b] * hd[b : b + 1, :]
        return 0

    lax.fori_loop(0, 2, last_event, 0)

    def combine(b, _):
        total = -e[1, b]
        for j in range(C):
            total = total - qb[j] * e[0, b, j : j + 1, :]
        w_ref[b] = total
        out_ref[b] = total
        return 0

    lax.fori_loop(0, S, combine, 0)

    store_split_v(w_ref)
    sndh[LAST, 0] = dot_nt(Pn[...], vcat[...])
    start(sndh, rcvh, hs, hr, (LAST, 0))
    rr_store(64, w_ref)
    left = jnp.concatenate([rr[64:80, :], rr[192:208, :]], axis=0)
    parts = dot_nt(left, rr[...])
    parts = parts[:, 0:128] + parts[:, 128:256]
    scale = 1.0 / (N * S * n_dom)
    ar_start(1, 0, (parts[0:16] + parts[16:32]) * scale)
    gather_local(vv.at[0])
    total = own(w_ref)
    for a in range(S):
        acc[0, a] = 0.5 * total[a]
    wait_recv(sndh, rcvh, hs, hr, (LAST, 0))
    gather_halo(rcvh[LAST, 0], vv.at[0])
    total = far(vv.at[0])
    for a in range(S):
        v[0, a] = acc[0, a] - total[a]
    rr_store(80, v.at[0])
    images = jnp.concatenate([rr[80:96, :], rr[208:224, :]], axis=0)
    parts = dot_nt(jnp.concatenate([left, images], axis=0), rr[...])
    parts = parts[:, 0:128] + parts[:, 128:256]
    first = pltpu.roll(parts[0:16] + parts[16:32], 128 - 80, 1)
    second = pltpu.roll(parts[32:48] + parts[48:64], 128 - 64, 1)
    lane = iota((C, 128), 1)
    both = jnp.where(lane < 16, first + second, 0.0) * scale
    small = both[0:8] + pltpu.roll(both[8:16], 16, 1)
    gram2[...] = ar_finish(1, 0)
    ar_start(1, 1, gram2[...])
    ar_start(2, 0, small)

    small = ar_finish(2, 0)
    ar_start(2, 1, small)
    gram2[...] = ar_finish(1, 1)

    def place(value, source, target):
        shift = (target - source) % 128
        moved = pltpu.roll(value, shift, 1) if shift else value
        return jnp.where((lane >= target) & (lane < target + 16), moved, 0.0)

    g1, g2 = gram1[...], gram2[...]
    turned = jnp.concatenate([g2, jnp.zeros((128 - C, 128), f32)], axis=0).T
    xw, pw, xaw, paw = [turned[16 * j : 16 * j + 16, :] for j in range(4)]
    gb_ref[0:16, :] = (place(g1, 0, 0) + place(xw, 0, 16) + place(g1, 16, 32))[:, 0:48]
    gb_ref[16:32, :] = (place(g2, 0, 0) + place(g2, 64, 16) + place(g2, 16, 32))[:, 0:48]
    gb_ref[32:48, :] = (place(g1, 64, 0) + place(pw, 0, 16) + place(g1, 80, 32))[:, 0:48]
    ga_ref[0:16, :] = (place(g1, 32, 0) + place(xaw, 0, 16) + place(g1, 48, 32))[:, 0:48]
    ga_ref[32:48, :] = (place(g1, 96, 0) + place(paw, 0, 16) + place(g1, 112, 32))[:, 0:48]
    wide = place(g2, 32, 0) + place(g2, 48, 32)
    small = ar_finish(2, 1)
    ww = jnp.concatenate([small, pltpu.roll(small, 128 - 16, 1)], axis=0)
    ga_ref[16:32, :] = (wide + place(ww, 0, 16))[:, 0:48]

    def drain(g, _):
        i, ch = lax.div(g, 2), lax.rem(g, 2)
        wait_send(sndh, rcvh, hs, hr, (i, ch))

        @pl.when((i != 3) & (i != 5))
        def _():
            wait_send(sndc, rcvc, cs, cr, (i, ch))

        return 0

    lax.fori_loop(0, 2 * LAST, drain, 0)
    wait_send(sndh, rcvh, hs, hr, (LAST, 0))
    wait_send(sndc, rcvc, cs, cr, (LAST, 0))
    wait_send(sndd, rcvd, ds, dr, ())
    for slot in range(3):
        for s in range(len(groups[slot])):
            ar_drain(slot, s)


def shards(n_dom, ar_dims, x, p, f_own, f_other, mass, cols, degree, send, pair, partner):
    vm = pltpu.VMEM
    dma = pltpu.SemaphoreType.DMA

    def size(dims):
        total = 1
        for _, g in dims:
            total *= g
        return total

    rows = (16, 16, 8)
    scratch = [
        vm((K, S, S, N), f32),
        vm((S, S, N), f32),
        vm((S, N), f32),
        vm((S, N), f32),
        vm((S, N), f32),
        vm((2, S, C, N), f32),
        vm((2, S, C, N), f32),
        vm((2, S, C, N), f32),
        vm((2, S, C, N), f32),
        vm((2, K, S, C, N), f32),
        vm((S, C, N), f32),
        vm((C, C, 128), f32),
        vm((C, 128), f32),
        vm((C, 128), f32),
        vm((S * C, T * N), bf16),
        vm((S * C, T * K * N), bf16),
        vm((256, S * N), bf16),
        vm((T * N, K * N), bf16),
        vm((H, T * K * N), bf16),
        vm((T * H, K * N), bf16),
        vm((T * K * N, N), bf16),
        vm((H, T * N), bf16),
        vm((T * H, N), bf16),
        vm((H, T * N), bf16),
        vm((T * N, N), bf16),
        vm((T * H, N), bf16),
        vm((LAST + 1, 2, H, S * C), f32),
        vm((LAST + 1, 2, H, S * C), f32),
        vm((LAST + 1, 2, H, S * C), f32),
        vm((LAST + 1, 2, H, S * C), f32),
        vm((H, 128), f32),
        vm((H, 128), f32),
        [[vm((size(d), rows[j], 128), f32) for d in st] for j, st in enumerate(ar_dims)],
        dma((LAST + 1, 2, 2)),
        dma((LAST + 1, 2, 2)),
        dma((LAST + 1, 2, 2)),
        dma((LAST + 1, 2, 2)),
        dma((2,)),
        dma((2,)),
        [[dma((size(d),)) for d in st] for st in ar_dims],
        [[dma((size(d),)) for d in st] for st in ar_dims],
    ]
    whole = pl.BlockSpec(memory_space=pltpu.VMEM)
    return pl.pallas_call(
        functools.partial(kernel, n_dom, ar_dims),
        out_shape=(
            jax.ShapeDtypeStruct((S, C, N), f32),
            jax.ShapeDtypeStruct((3 * C, 3 * C), f32),
            jax.ShapeDtypeStruct((3 * C, 3 * C), f32),
        ),
        in_specs=[whole] * 10,
        out_specs=(whole, whole, whole),
        scratch_shapes=scratch,
        compiler_params=pltpu.CompilerParams(
            collective_id=0, has_side_effects=True, vmem_limit_bytes=48 * 1024 * 1024
        ),
    )(
        x, p, f_own, f_other, mass, cols,
        degree.reshape(1, N), send.reshape(1, H), pair.reshape(1, H), partner.reshape(1, N),
    )


def solution(mesh):
    n_dom = mesh.shape["dom"]
    if n_dom == 512:
        near = [[(1, 8)], [(128, 4)], [(8, 4)], [(32, 4)]]
        quick = [[(128, 4), (1, 8)], [(8, 16)]]
    else:
        near = [[(1, 2)], [(2, n_dom // 2)]]
        quick = [[(1, 2)], [(2, n_dom // 2)]]
    row = P(None, "dom")
    return jax.shard_map(
        functools.partial(shards, n_dom, (near, quick, quick)),
        mesh=mesh,
        in_specs=(
            P(None, None, "dom"),
            P(None, None, "dom"),
            P(None, None, None, "dom"),
            P(None, None, None, "dom"),
            row, row, P("dom"), P("dom"), P("dom"), P("dom"),
        ),
        out_specs=(P(None, None, "dom"), P(), P()),
        check_vma=False,
    )
```

time: 924 us -> 101 us (0.11)
  other arithmetic: 380 us -> 0 us
  blocking collectives: 223 us -> 0 us
  starting transfers between devices: 179 us -> 0 us
  local copies, waits for them, and re-layouts: 122 us -> 7.14 us
  Pallas kernels: 0 us -> 92.5 us
    scatter-add x16 -> x0, other arithmetic: 296 us -> none  [the longest x7 281 us: edge_terms(): gathered = jnp.zeros(extended.shape, jnp.float32).at[:, :, block_cols].ad...]
    psum x2 -> x0, blocking collectives: 223 us -> none  [the longest x1 113 us: shards(): lax.psum((gram_block(basis, images, norm_scale), gram_block(basis, basis,...]
    ppermute x32 -> x0, starting transfers between devices: 179 us -> none  [the longest x16 146 us: extended_2(): after = lax.ppermute(first, axis, down)]
    pallas_call x0 -> x1, Pallas kernels: none -> 92.5 us  [shards(): pl.pallas_call(functools.partial(kernel, n_dom, ar_dims), out_shape=(jax....]
    gather x27 -> x0, local copies, waits for them, and re-layouts: 33.5 us -> none  [the longest x7 21.4 us: edge_terms(): remote = jnp.moveaxis(jnp.take(extended, block_cols, axis=2), 2, 0)]
    reduce_sum x22 -> x0, other arithmetic: 33.1 us -> none  [the longest x7 13.3 us: edge_terms(): jnp.sum(f_other[:, :, :, None, :] * mismatch[:, :, None, :, :], axis=1)]
    transpose x6 -> x0, other arithmetic: 23.5 us -> none  [edge_terms(): remote = jnp.moveaxis(jnp.take(extended, block_cols, axis=2), 2, 0)]
    neg x7 -> x0, local copies, waits for them, and re-layouts: 19.8 us -> none  [edge_terms(): -jnp.moveaxis(far_part, 0, 2)]
  transfers between devices with their start and end apart: 32 -> 0, of which waited for: 2 -> 0; matrix products, arithmetic and copies ran while one was open for 4% -> 0% of each run, Pallas kernels for 0% -> 0%
where the time goes in v1:
time: 101 us; the launch traced here: 100 us
  Pallas kernels  92.5 us (92%)
  local copies, waits for them, and re-layouts  7.14 us (7%)
    pallas_call x1, Pallas kernels, shards(): pl.pallas_call(functools.partial(kernel, n_dom, ar_dims), out_shape=(jax....  92.5 us
    unnamed x23, local copies, waits for them, and re-layouts  7.14 us

profile of v1, /device:TPU:1, one launch (start us, length us, event | category | flops | bytes accessed | tf_op | source)
XLA Modules:
  0.0 100.3 jit_solution(18249686075407139819)
XLA Ops:
  0.6 0.0 copy-start.9
  0.6 0.0 copy-start.5
  0.7 0.0 copy-start.6
  0.7 0.0 copy-start.7
  0.7 0.0 copy-start.8
  0.7 0.6 copy-done.9
  1.3 0.0 copy-done.5
  1.3 0.0 copy-done.6
  1.3 0.0 copy-done.7
  1.3 0.0 copy-done.8
  1.4 0.0 copy-start
  1.4 1.0 %copy-done = f32[4,16,16,128]{3,2,1,0:T(8,128)S(1)} copy-done((f32[4,16,16,128]{3,2,1,0:T(8,128)S(1)}, f32[4,16,16,128]{3,2,1,0:T(8,128)}, u32[]{:S(2)}) %copy-start) | copy-done | bytes 524312
  2.4 0.0 copy-start.1
  2.4 1.0 %copy-done.1 = f32[4,16,16,128]{3,2,1,0:T(8,128)S(1)} copy-done((f32[4,16,16,128]{3,2,1,0:T(8,128)S(1)}, f32[4,16,16,128]{3,2,1,0:T(8,128)}, u32[]{:S(2)}) %copy-start.1) | copy-done | bytes 524312
  3.4 0.0 copy-start.2
  3.4 0.9 copy-done.2
  4.3 0.0 copy-start.3
  4.3 0.9 copy-done.3
  5.2 0.0 copy-start.4
  5.2 0.7 copy-done.4
  5.9 92.5 %shard_map.121 = (f32[16,16,128]{2,1,0:T(8,128)S(1)}, f32[48,48]{1,0:T(8,128)S(1)}, f32[48,48]{1,0:T(8,128)S(1)}) custom-call(f32[16,16,128]{2,1,0:T(8,128)S(1)} %copy-done.2, f32[16,16,128]{2,1,0:T(8,128)S(1)} %copy-done.3, f32[4,16,16,128]{3,2,1,0:T(8,128)S(1)} %copy-done, f32[4,16,16,128]{3,2,1,0:T(8,128)S(1)} %copy-done.1, f32[16,128]{1,0:T(8,128)S(1)} %copy-done.4, ...), custom_call_target="tpu_custom_call" | custom-call | tf_op jit(solution)/shard_map/pallas_call | solution.py:597
  98.5 0.7 copy.16
  99.1 0.6 copy.17
  99.7 0.6 copy.18
Async XLA Ops:
  0.6 0.7 copy-start.9
  0.6 0.7 copy-start.5
  0.7 0.7 copy-start.6
  0.7 0.7 copy-start.7
  0.7 0.7 copy-start.8
  1.4 1.0 %copy-start = (f32[4,16,16,128]{3,2,1,0:T(8,128)S(1)}, f32[4,16,16,128]{3,2,1,0:T(8,128)}, u32[]{:S(2)}) copy-start(f32[4,16,16,128]{3,2,1,0:T(8,128)} %own_ref.1) | copy-start | bytes 1572868
  2.4 1.0 %copy-start.1 = (f32[4,16,16,128]{3,2,1,0:T(8,128)S(1)}, f32[4,16,16,128]{3,2,1,0:T(8,128)}, u32[]{:S(2)}) copy-start(f32[4,16,16,128]{3,2,1,0:T(8,128)} %oth_ref.1) | copy-start | bytes 1572868
  3.4 0.9 copy-start.2
  4.3 0.9 copy-start.3
  5.2 0.7 copy-start.4

commit v2 on v1

--- a/solution.py
+++ b/solution.py
@@ -75,12 +75,13 @@
 
 def kernel(
     n_dom, ar_dims,
-    x_ref, p_ref, own_ref, oth_ref, mass_ref, cols_ref, deg_ref, send_ref, pair_ref, part_ref,
+    x_in, p_in, own_in, oth_in, mass_in, cols_in, deg_in, send_in, pair_in, part_in,
     out_ref, ga_ref, gb_ref,
+    x_ref, p_ref, own_ref, oth_ref, mass_ref, cols_ref, deg_ref, send_ref, pair_ref, part_ref, in_sems,
     B, D, hd, hdc, diag, v, y, e, acc, vv, w_ref, qb, gram1, gram2,
-    vcat, wcat, rr, Gl, GH, GHs, ST, Pn, Pr, PPn, Ql, Qh,
+    vcat, wcat, rr, Gl, GS, GHs, Pn, Pr, Ql, Qh, raw,
     sndh, rcvh, sndc, rcvc, sndd, rcvd, ar_bufs,
-    hs, hr, cs, cr, ds, dr, ar_ss, ar_rs,
+    hs, hr, cs, cr, ds, dr, ar_ss, ar_rs, vouched,
 ):
     me = lax.axis_index("dom")
     lower = lax.rem(me + n_dom - 1, n_dom)
@@ -91,15 +92,35 @@
     barrier = pltpu.get_barrier_semaphore()
     for d in (lower, upper):
         pl.semaphore_signal(barrier, inc=1, device_id=(d,), device_id_type=MESH)
-    n_bar = 2
-    for g in bar_groups:
-        n_bar += g.size - 1
-
-        def greet(t, _, g=g):
-            pl.semaphore_signal(barrier, inc=1, device_id=(g.device(g.peer(t)),), device_id_type=MESH)
-            return 0
-
-        lax.fori_loop(1, g.size, greet, 0)
+    wide, ring = bar_groups
+    reach = 4
+    n_bar = 2 + wide.size - 1 + 2 * reach
+
+    def greet(g, t):
+        pl.semaphore_signal(barrier, inc=1, device_id=(g.device(g.peer(t)),), device_id_type=MESH)
+
+    def greet_wide(t, _):
+        greet(wide, t)
+        return 0
+
+    for t in range(reach, 0, -1):
+        greet(ring, t)
+        greet(ring, ring.size - t)
+    lax.fori_loop(1, wide.size, greet_wide, 0)
+
+    def vouch():
+        for j, t in enumerate((reach, ring.size - reach)):
+            pl.semaphore_signal(
+                vouched.at[j], inc=1, device_id=(ring.device(ring.peer(t)),), device_id_type=MESH
+            )
+
+    def fetch(j):
+        src = (x_in, p_in, own_in, oth_in, mass_in, cols_in, deg_in, send_in, pair_in, part_in)[j]
+        dst = (x_ref, p_ref, own_ref, oth_ref, mass_ref, cols_ref, deg_ref, send_ref, pair_ref, part_ref)[j]
+        return pltpu.make_async_copy(src, dst, in_sems.at[j])
+
+    for j in (5, 9, 7, 8, 6, 3, 2, 0, 1, 4):
+        fetch(j).start()
 
     def pair_copies(snd, rcv, ss, rs, idx):
         out = []
@@ -175,16 +196,16 @@
 
         lax.fori_loop(1, g.size, go, 0)
 
+    for j in (5, 9, 7, 8, 6):
+        fetch(j).wait()
     for k in range(K):
         at_k = pl.ds(k * N, N)
-        hot = one_hot(iota((N, N), 0) == cols_ref[k : k + 1, :])
-        hot_t = hot.T.astype(bf16)
+        hot = one_hot(iota((N, N), 0) == cols_ref[k : k + 1, :]).astype(bf16)
         halo = one_hot(iota((H, N), 0) + N == cols_ref[k : k + 1, :]).astype(bf16)
-        hot = hot.astype(bf16)
         for t in range(T):
             Gl[pl.ds(t * N, N), at_k] = hot
-            ST[pl.ds((t * K + k) * N, N), :] = hot_t
-            GH[:, pl.ds((t * K + k) * N, N)] = halo
+            GS[0:N, pl.ds((k * T + t) * N, N)] = hot
+            GS[N : N + H, pl.ds((k * T + t) * N, N)] = halo
             GHs[pl.ds(t * H, H), at_k] = halo
     hot = one_hot(iota((N, N), 0) == part_ref[...]).astype(bf16)
     halo = one_hot(iota((H, N), 0) + N == part_ref[...]).astype(bf16)
@@ -200,33 +221,36 @@
     sel = one_hot(lanes == column(send_ref)).astype(bf16)
     psel = one_hot(lanes == column(pair_ref)).astype(bf16)
     for t in range(T):
-        Pn[:, pl.ds(t * N, N)] = sel
+        Pn[0, :, pl.ds(t * N, N)] = sel
+        Pn[1, :, pl.ds(t * N, N)] = psel
         Pr[pl.ds(t * H, H), :] = sel
-        PPn[:, pl.ds(t * N, N)] = psel
 
     def bcast_rows(ref, idx, r):
         return ref[idx + (slice(r, r + 1), slice(None))]
 
     def store_split_w(k, b, value):
         for t, term in enumerate(split(value)):
-            wcat[pl.ds(b * C, C), pl.ds(pl.multiple_of(t * K * N + k * N, N), N)] = term
+            wcat[pl.ds(b * C, C), pl.ds((k * T + t) * N, N)] = term
 
     def store_split_v(ref):
         for b in range(S):
             for t, term in enumerate(split(ref[b])):
                 vcat[pl.ds(b * C, C), pl.ds(t * N, N)] = term
 
-    def scatter_halo():
-        return dot_nt(GH[...], wcat[...])
-
-    def scatter_local():
-        return dot_nn(wcat[...], ST[...])
+    def scatter_slot(k, total):
+        at_k = slice(k * T * N, (k + 1) * T * N)
+        part = dot_nt(GS[:, at_k], wcat[:, at_k])
+        return part if total is None else total + part
+
+    def turned_rows(rows):
+        return jnp.concatenate([rows[0:N, 0:N].T, rows[0:N, N : 2 * N].T], axis=0).reshape(S, C, N)
 
     def from_halo(rows, matrix):
         return dot_tn(jnp.concatenate(split(rows), axis=0), matrix[...])
 
     def reverse(ref):
-        def body(k, _):
+        rows = None
+        for k in range(K):
             for half in range(2):
                 total = [jnp.zeros((C, N), f32)] * 8
                 for a in range(S):
@@ -235,22 +259,26 @@
                         total[j] = total[j] + bcast_rows(B, (k, a), half * 8 + j) * value
                 for j in range(8):
                     store_split_w(k, half * 8 + j, total[j])
-            return 0
-
-        lax.fori_loop(0, K, body, 0)
-
-    def far(src):
-        def body(k, total):
-            total = list(total)
+            rows = scatter_slot(k, rows)
+        return rows
+
+    def far(near, rows, half_way=None):
+        rows = jnp.concatenate(split(rows), axis=0).T
+        total = [jnp.zeros((C, N), f32)] * S
+        for k in range(K):
+            if k % 2 == 0:
+                got = dot_nn(rows, GHs[:, k * N : (k + 2) * N])
+            if k == 2 and half_way is not None:
+                half_way()
+            part = got[:, (k % 2) * N : (k % 2 + 1) * N].reshape(S, C, N)
+            near[k] = near[k] + part
             for b in range(S):
-                value = src[k, b]
+                value = near[k, b]
                 for a in range(S):
                     total[a] = total[a] + bcast_rows(B, (k, a), b) * value
-            return tuple(total)
-
-        return lax.fori_loop(0, K, body, tuple(jnp.zeros((C, N), f32) for _ in range(S)))
-
-    def own(ref, factor=None):
+        return total
+
+    def own(ref, D):
         total = [jnp.zeros((C, N), f32)] * S
         for b in range(S):
             value = ref[b]
@@ -263,56 +291,62 @@
         for k in range(K):
             dst[k] = rows[:, k * N : (k + 1) * N].reshape(S, C, N)
 
-    def gather_halo(rows, dst):
-        got = from_halo(rows, GHs)
-        for k in range(K):
-            dst[k] = dst[k] + got[:, k * N : (k + 1) * N].reshape(S, C, N)
-
-    def a_start(i, ch, with_own=True):
+    def send_rows(i, ch, which):
+        sndh[i, ch] = dot_nt(Pn[which], vcat[...])
+        start(sndh, rcvh, hs, hr, (i, ch))
+
+    def a_rest(i, ch, enter=None):
         src = v.at[ch]
-        store_split_v(src)
-        sndh[i, ch] = dot_nt(Pn[...], vcat[...])
-        start(sndh, rcvh, hs, hr, (i, ch))
-        reverse(src)
-        sndc[i, ch] = scatter_halo()
+        rows = reverse(src)
+        sndc[i, ch] = rows[N : N + H]
+        if enter is not None:
+            enter()
         start(sndc, rcvc, cs, cr, (i, ch))
-        back = scatter_local().reshape(S, C, N)
         gather_local(vv.at[ch])
-        if with_own:
-            total = own(src)
-            for a in range(S):
-                acc[ch, a] = total[a] - back[a]
-        else:
-            acc[ch] = -back
+        back = turned_rows(rows)
+        total = own(src, D)
+        for a in range(S):
+            acc[ch, a] = total[a] - back[a]
 
     def a_finish(i, ch):
         wait_recv(sndh, rcvh, hs, hr, (i, ch))
-        gather_halo(rcvh[i, ch], vv.at[ch])
-        total = far(vv.at[ch])
-        wait_recv(sndc, rcvc, cs, cr, (i, ch))
+        total = far(
+            vv.at[ch], rcvh[i, ch], lambda: wait_recv(sndc, rcvc, cs, cr, (i, ch))
+        )
         got = from_halo(rcvc[i, ch], Pr).reshape(S, C, N)
-        for a in range(S):
-            y[ch, a] = y[ch, a] - acc[ch, a] + total[a] + got[a]
-
-    def q_start(i, ch):
-        store_split_v(y.at[ch])
-        sndh[i, ch] = dot_nt(PPn[...], vcat[...])
-        start(sndh, rcvh, hs, hr, (i, ch))
-        acc[ch] = y[ch] + dot_nn(vcat[...], Ql[...]).reshape(S, C, N)
-
-    def q_finish(i, ch):
-        wait_recv(sndh, rcvh, hs, hr, (i, ch))
-        got = from_halo(rcvh[i, ch], Qh).reshape(S, C, N)
+        return [y[ch, a] - acc[ch, a] + got[a] + total[a] for a in range(S)]
+
+    def split_pair(b, value):
+        for t, term in enumerate(split(value)):
+            vcat[pl.ds(b * C, C), pl.ds(t * N, N)] = term
+
+    def after_a(i, ch, coarse_start):
+        first = i == 1
+        which = coarse_start.astype(jnp.int32)
+        scale = jnp.where(coarse_start, 1.0, hd[...])
+        keep = jnp.where(coarse_start, 0.0, 1.0)
+        for b, value in enumerate(a_finish(i - 1, ch)):
+            raw[b] = value
+            value = jnp.where(first & (ch == 0), x_ref[b], value)
+            y[ch, b] = value
+            value = value * scale[b : b + 1, :]
+            v[ch, b] = value
+            e[ch, b] = e[ch, b] + keep * value
+            split_pair(b, value)
+        send_rows(i, ch, which)
+
+    def after_q(i, ch):
+        wait_recv(sndh, rcvh, hs, hr, (i - 1, ch))
+        got = from_halo(rcvh[i - 1, ch], Qh).reshape(S, C, N)
         for b in range(S):
             value = (acc[ch, b] + got[b]) * hdc[b : b + 1, :]
             v[ch, b] = value
             e[ch, b] = e[ch, b] + value
-
-    def smooth(ch):
-        for b in range(S):
-            value = y[ch, b] * hd[b : b + 1, :]
-            v[ch, b] = value
-            e[ch, b] = e[ch, b] + value
+            split_pair(b, value)
+        send_rows(i, ch, 0)
+
+    def q_rest(ch):
+        acc[ch] = y[ch] + dot_nn(vcat[...], Ql[...]).reshape(S, C, N)
 
     def rr_store(row, ref, sign=1.0):
         for b in range(S):
@@ -329,44 +363,64 @@
         return lax.fori_loop(0, S, body, tuple(jnp.zeros((S, N), f32) for _ in range(S)), unroll=4)
 
     rr[...] = jnp.zeros_like(rr)
+    e[...] = jnp.zeros_like(e)
+    y[...] = jnp.zeros_like(y)
+    fetch(3).wait()
+    rows = None
     for k in range(K):
         for a, value in enumerate(outer(oth_ref, oth_ref, k)):
             store_split_w(k, a, value * live[k])
-    sndc[LAST, 0] = scatter_halo()
-    D[...] = scatter_local().reshape(S, S, N)
+        rows = scatter_slot(k, rows)
+    sndc[LAST, 0] = rows[N : N + H]
+    D[...] = turned_rows(rows)
+    fetch(2).wait()
+    for k in range(K):
+        for a, value in enumerate(outer(own_ref, oth_ref, k)):
+            B[k, a] = value * live[k]
+    fetch(0).wait()
+    v[1] = x_ref[...]
+
+    def enter():
+        pl.semaphore_wait(barrier, n_bar)
+        vouch()
+        start(sndc, rcvc, cs, cr, (LAST, 0))
+
     for k in range(K):
         for a, value in enumerate(outer(own_ref, own_ref, k)):
             D[a] = D[a] + value * live[k]
-        for a, value in enumerate(outer(own_ref, oth_ref, k)):
-            B[k, a] = value * live[k]
+    fetch(4).wait()
     for b in range(S):
         D[b, b : b + 1, :] = D[b, b : b + 1, :] + mass_ref[b : b + 1, :]
-    e[...] = jnp.zeros_like(e)
-    y[...] = jnp.zeros_like(y)
+    store_split_v(x_ref)
+    sndh[0, 1] = dot_nt(Pn[0], vcat[...])
+
+    def enter_and_send():
+        enter()
+        start(sndh, rcvh, hs, hr, (0, 1))
+
+    a_rest(0, 1, enter_and_send)
+    fetch(1).wait()
     v[0] = p_ref[...]
-    v[1] = x_ref[...]
+    store_split_v(p_ref)
+    send_rows(0, 0, 0)
+    a_rest(0, 0)
     rr_store(0, x_ref)
     rr_store(16, p_ref)
 
-    pl.semaphore_wait(barrier, n_bar)
-
-    start(sndc, rcvc, cs, cr, (LAST, 0))
-    a_start(0, 1, False)
-    a_start(0, 0, False)
-
     wait_recv(sndc, rcvc, cs, cr, (LAST, 0))
-    D[...] = D[...] + from_halo(rcvc[LAST, 0], Pr).reshape(S, S, N)
+    w_ref[...] = from_halo(rcvc[LAST, 0], Pr).reshape(S, S, N)
+    for ch in (1, 0):
+        total = own(v.at[ch], w_ref)
+        for a in range(S):
+            acc[ch, a] = acc[ch, a] + total[a]
+    D[...] = D[...] + w_ref[...]
     for b in range(S):
         diag[b : b + 1, :] = D[b, b : b + 1, :]
     hd[...] = 0.5 / diag[...]
     dcat = jnp.concatenate(split(diag[...]), axis=1)
     sndd[...] = jnp.zeros_like(sndd)
-    sndd[:, 0:S] = dot_nt(PPn[...], dcat)
+    sndd[:, 0:S] = dot_nt(Pn[1], dcat)
     start(sndd, rcvd, ds, dr, ())
-    for ch in (1, 0):
-        total = own(v.at[ch])
-        for a in range(S):
-            acc[ch, a] = acc[ch, a] + total[a]
 
     def event(g, _):
         i = 1 + lax.div(g, 2)
@@ -376,32 +430,27 @@
 
         @pl.when(jnp.logical_not(coarse_end))
         def _():
-            a_finish(i - 1, ch)
+            after_a(i, ch, coarse_start)
+
+        @pl.when(coarse_end)
+        def _():
+            after_q(i, ch)
+
+        @pl.when(coarse_start)
+        def _():
+            q_rest(ch)
+
+        @pl.when(jnp.logical_not(coarse_start))
+        def _():
+            a_rest(i, ch)
 
         @pl.when((i == 1) & (ch == 1))
         def _():
-            rr_store(32, y.at[1], -1.0)
+            rr_store(32, raw, -1.0)
 
         @pl.when((i == 1) & (ch == 0))
         def _():
-            rr_store(48, y.at[0], -1.0)
-            y[0] = x_ref[...]
-
-        @pl.when(coarse_end)
-        def _():
-            q_finish(i - 1, ch)
-
-        @pl.when(jnp.logical_not(coarse_end | coarse_start))
-        def _():
-            smooth(ch)
-
-        @pl.when(coarse_start)
-        def _():
-            q_start(i, ch)
-
-        @pl.when(jnp.logical_not(coarse_start))
-        def _():
-            a_start(i, ch)
+            rr_store(48, raw, -1.0)
 
         late = ch == 0
 
@@ -413,6 +462,8 @@
             parts = (parts[0:32] + parts[32:64]) * (1.0 / (N * S * n_dom))
             rolled = pltpu.roll(parts[16:32], 64, 1)
             ar_start(0, 0, jnp.where(iota((C, 128), 1) < 64, parts[0:16], rolled))
+            for j in range(2):
+                pl.semaphore_wait(vouched.at[j], 1)
 
         @pl.when(late & (i == 2))
         def _():
@@ -450,9 +501,8 @@
 
     def last_event(g, _):
         ch = g
-        a_finish(LAST - 1, ch)
-        for b in range(S):
-            e[ch, b] = e[ch, b] + y[ch, b] * hd[b : b + 1, :]
+        for b, value in enumerate(a_finish(LAST - 1, ch)):
+            e[ch, b] = e[ch, b] + value * hd[b : b + 1, :]
         return 0
 
     lax.fori_loop(0, 2, last_event, 0)
@@ -462,81 +512,106 @@
         for j in range(C):
             total = total - qb[j] * e[0, b, j : j + 1, :]
         w_ref[b] = total
-        out_ref[b] = total
         return 0
 
     lax.fori_loop(0, S, combine, 0)
 
+    result = pltpu.make_async_copy(w_ref, out_ref, in_sems.at[10])
+    result.start()
     store_split_v(w_ref)
-    sndh[LAST, 0] = dot_nt(Pn[...], vcat[...])
+    sndh[LAST, 0] = dot_nt(Pn[0], vcat[...])
     start(sndh, rcvh, hs, hr, (LAST, 0))
     rr_store(64, w_ref)
+    lane = iota((C, 128), 1)
+    scale = 1.0 / (N * S * n_dom)
     left = jnp.concatenate([rr[64:80, :], rr[192:208, :]], axis=0)
     parts = dot_nt(left, rr[...])
-    parts = parts[:, 0:128] + parts[:, 128:256]
-    scale = 1.0 / (N * S * n_dom)
-    ar_start(1, 0, (parts[0:16] + parts[16:32]) * scale)
+    parts = (parts[0:16, 0:128] + parts[0:16, 128:256] + parts[16:32, 0:128] + parts[16:32, 128:256]) * scale
+    low = jnp.where(lane < 64, parts, 0.0)
+    ar_start(1, 0, low[0:8] + pltpu.roll(low[8:16], 64, 1))
+
+    diagonal = lax.div(lane, 16) == lax.rem(iota((C, 128), 0), 8)
+
+    def pack_block(block):
+        for shift in (16, 32, 64):
+            block = block + pltpu.roll(block, shift, 1)
+        block = jnp.where(diagonal, block, 0.0)
+        top = jnp.sum(block[0:8], axis=0, keepdims=True)
+        return jnp.concatenate([top, jnp.sum(block[8:16], axis=0, keepdims=True)], axis=0)
+
+    def unpack_block(pair):
+        wide = jnp.concatenate(
+            [jnp.broadcast_to(pair[0:1], (8, 128)), jnp.broadcast_to(pair[1:2], (8, 128))], axis=0
+        )
+        wide = jnp.where(diagonal, wide, 0.0)
+        for shift in (16, 32, 64):
+            wide = wide + pltpu.roll(wide, shift, 1)
+        return wide
+
+    def lanes_from(value, source):
+        return jnp.where(lane < 16, pltpu.roll(value, 128 - source, 1), 0.0)
+
+    gram2[0:2, :] = pack_block(lanes_from(parts, 64))
     gather_local(vv.at[0])
-    total = own(w_ref)
+    total = own(w_ref, D)
     for a in range(S):
         acc[0, a] = 0.5 * total[a]
     wait_recv(sndh, rcvh, hs, hr, (LAST, 0))
-    gather_halo(rcvh[LAST, 0], vv.at[0])
-    total = far(vv.at[0])
+    total = far(vv.at[0], rcvh[LAST, 0])
     for a in range(S):
         v[0, a] = acc[0, a] - total[a]
     rr_store(80, v.at[0])
     images = jnp.concatenate([rr[80:96, :], rr[208:224, :]], axis=0)
+    left = jnp.concatenate([rr[64:80, :], rr[192:208, :]], axis=0)
     parts = dot_nt(jnp.concatenate([left, images], axis=0), rr[...])
     parts = parts[:, 0:128] + parts[:, 128:256]
-    first = pltpu.roll(parts[0:16] + parts[16:32], 128 - 80, 1)
-    second = pltpu.roll(parts[32:48] + parts[48:64], 128 - 64, 1)
-    lane = iota((C, 128), 1)
-    both = jnp.where(lane < 16, first + second, 0.0) * scale
-    small = both[0:8] + pltpu.roll(both[8:16], 16, 1)
-    gram2[...] = ar_finish(1, 0)
-    ar_start(1, 1, gram2[...])
-    ar_start(2, 0, small)
-
-    small = ar_finish(2, 0)
-    ar_start(2, 1, small)
-    gram2[...] = ar_finish(1, 1)
+    both = lanes_from(parts[0:16] + parts[16:32], 80) + lanes_from(parts[32:48] + parts[48:64], 64)
+    ar_start(2, 0, jnp.concatenate([pack_block(both * scale), gram2[0:2, :]], axis=0))
+
+    def drain(g, _):
+        i, ch = lax.div(g, 2), lax.rem(g, 2)
+        wait_send(sndh, rcvh, hs, hr, (i, ch))
+
+        @pl.when((i != 3) & (i != 5))
+        def _():
+            wait_send(sndc, rcvc, cs, cr, (i, ch))
+
+        return 0
+
+    ar_start(1, 1, ar_finish(1, 0))
+    lax.fori_loop(0, 2 * LAST, drain, 0)
+    wait_send(sndh, rcvh, hs, hr, (LAST, 0))
+    wait_send(sndc, rcvc, cs, cr, (LAST, 0))
+    wait_send(sndd, rcvd, ds, dr, ())
+    ar_start(2, 1, ar_finish(2, 0))
+    for s in range(len(groups[0])):
+        ar_drain(0, s)
+    ar_drain(1, 0)
+    ar_drain(2, 0)
+    half = ar_finish(1, 1)
+    high = pltpu.roll(half, 64, 1)
+    g2 = jnp.where(lane < 64, jnp.concatenate([half, high], axis=0), 0.0)
 
     def place(value, source, target):
         shift = (target - source) % 128
         moved = pltpu.roll(value, shift, 1) if shift else value
         return jnp.where((lane >= target) & (lane < target + 16), moved, 0.0)
 
-    g1, g2 = gram1[...], gram2[...]
+    g1 = gram1[...]
     turned = jnp.concatenate([g2, jnp.zeros((128 - C, 128), f32)], axis=0).T
     xw, pw, xaw, paw = [turned[16 * j : 16 * j + 16, :] for j in range(4)]
     gb_ref[0:16, :] = (place(g1, 0, 0) + place(xw, 0, 16) + place(g1, 16, 32))[:, 0:48]
-    gb_ref[16:32, :] = (place(g2, 0, 0) + place(g2, 64, 16) + place(g2, 16, 32))[:, 0:48]
     gb_ref[32:48, :] = (place(g1, 64, 0) + place(pw, 0, 16) + place(g1, 80, 32))[:, 0:48]
     ga_ref[0:16, :] = (place(g1, 32, 0) + place(xaw, 0, 16) + place(g1, 48, 32))[:, 0:48]
     ga_ref[32:48, :] = (place(g1, 96, 0) + place(paw, 0, 16) + place(g1, 112, 32))[:, 0:48]
-    wide = place(g2, 32, 0) + place(g2, 48, 32)
-    small = ar_finish(2, 1)
-    ww = jnp.concatenate([small, pltpu.roll(small, 128 - 16, 1)], axis=0)
-    ga_ref[16:32, :] = (wide + place(ww, 0, 16))[:, 0:48]
-
-    def drain(g, _):
-        i, ch = lax.div(g, 2), lax.rem(g, 2)
-        wait_send(sndh, rcvh, hs, hr, (i, ch))
-
-        @pl.when((i != 3) & (i != 5))
-        def _():
-            wait_send(sndc, rcvc, cs, cr, (i, ch))
-
-        return 0
-
-    lax.fori_loop(0, 2 * LAST, drain, 0)
-    wait_send(sndh, rcvh, hs, hr, (LAST, 0))
-    wait_send(sndc, rcvc, cs, cr, (LAST, 0))
-    wait_send(sndd, rcvd, ds, dr, ())
-    for slot in range(3):
-        for s in range(len(groups[slot])):
-            ar_drain(slot, s)
+    wide_a = place(g2, 32, 0) + place(g2, 48, 32)
+    wide_b = place(g2, 0, 0) + place(g2, 16, 32)
+    ar_drain(1, 1)
+    last = ar_finish(2, 1)
+    ga_ref[16:32, :] = (wide_a + place(unpack_block(last[0:2]), 16, 16))[:, 0:48]
+    gb_ref[16:32, :] = (wide_b + place(unpack_block(last[2:4]), 16, 16))[:, 0:48]
+    ar_drain(2, 1)
+    result.wait()
 
 
 def shards(n_dom, ar_dims, x, p, f_own, f_other, mass, cols, degree, send, pair, partner):
@@ -549,8 +624,20 @@
             total *= g
         return total
 
-    rows = (16, 16, 8)
+    rows = (16, 8, 4)
+    i32 = jnp.int32
     scratch = [
+        vm((S, C, N), f32),
+        vm((S, C, N), f32),
+        vm((K, S, S, N), f32),
+        vm((K, S, S, N), f32),
+        vm((S, N), f32),
+        vm((K, N), i32),
+        vm((1, N), i32),
+        vm((1, H), i32),
+        vm((1, H), i32),
+        vm((1, N), i32),
+        dma((11,)),
         vm((K, S, S, N), f32),
         vm((S, S, N), f32),
         vm((S, N), f32),
@@ -569,14 +656,13 @@
         vm((S * C, T * K * N), bf16),
         vm((256, S * N), bf16),
         vm((T * N, K * N), bf16),
-        vm((H, T * K * N), bf16),
+        vm((N + H, T * K * N), bf16),
         vm((T * H, K * N), bf16),
-        vm((T * K * N, N), bf16),
-        vm((H, T * N), bf16),
+        vm((2, H, T * N), bf16),
         vm((T * H, N), bf16),
-        vm((H, T * N), bf16),
         vm((T * N, N), bf16),
         vm((T * H, N), bf16),
+        vm((S, C, N), f32),
         vm((LAST + 1, 2, H, S * C), f32),
         vm((LAST + 1, 2, H, S * C), f32),
         vm((LAST + 1, 2, H, S * C), f32),
@@ -592,6 +678,7 @@
         dma((2,)),
         [[dma((size(d),)) for d in st] for st in ar_dims],
         [[dma((size(d),)) for d in st] for st in ar_dims],
+        pltpu.SemaphoreType.REGULAR((2,)),
     ]
     whole = pl.BlockSpec(memory_space=pltpu.VMEM)
     return pl.pallas_call(
@@ -601,11 +688,11 @@
             jax.ShapeDtypeStruct((3 * C, 3 * C), f32),
             jax.ShapeDtypeStruct((3 * C, 3 * C), f32),
         ),
-        in_specs=[whole] * 10,
-        out_specs=(whole, whole, whole),
+        in_specs=[pl.BlockSpec(memory_space=pl.ANY)] * 10,
+        out_specs=(pl.BlockSpec(memory_space=pl.ANY), whole, whole),
         scratch_shapes=scratch,
         compiler_params=pltpu.CompilerParams(
-            collective_id=0, has_side_effects=True, vmem_limit_bytes=48 * 1024 * 1024
+            collective_id=0, has_side_effects=True, vmem_limit_bytes=56 * 1024 * 1024
         ),
     )(
         x, p, f_own, f_other, mass, cols,

time: 101 us -> 93.1 us (0.922)
  local copies, waits for them, and re-layouts: 7.14 us -> 2.93 us
  Pallas kernels: 92.5 us -> 89.3 us
    unnamed x23 -> x7, local copies, waits for them, and re-layouts: 7.14 us -> 2.93 us
    pallas_call x1, Pallas kernels: 92.5 us -> 89.3 us  [shards(): pl.pallas_call(functools.partial(kernel, n_dom, ar_dims), out_shape=(jax....]
where the time goes in v2:
time: 93.1 us; the launch traced here: 92.8 us
  Pallas kernels  89.3 us (96%)
  local copies, waits for them, and re-layouts  2.93 us (3%)
    pallas_call x1, Pallas kernels, shards(): pl.pallas_call(functools.partial(kernel, n_dom, ar_dims), out_shape=(jax....  89.3 us
    unnamed x7, local copies, waits for them, and re-layouts  2.93 us

profile of v2, /device:TPU:1, one launch (start us, length us, event | category | flops | bytes accessed | tf_op | source)
XLA Modules:
  0.0 92.8 jit_solution(17342162829906254145)
XLA Ops:
  0.6 89.3 %shard_map.121 = (f32[16,16,128]{2,1,0:T(8,128)}, f32[48,48]{1,0:T(8,128)}, f32[48,48]{1,0:T(8,128)}) custom-call(f32[16,16,128]{2,1,0:T(8,128)} %x_in.1, f32[16,16,128]{2,1,0:T(8,128)} %p_in.1, f32[4,16,16,128]{3,2,1,0:T(8,128)} %own_in.1, f32[4,16,16,128]{3,2,1,0:T(8,128)} %oth_in.1, f32[16,128]{1,0:T(8,128)} %mass_in.1, s32[4,128]{1,0:T(4,128)} %cols_in.1, ...), custom_call_target="tpu_custom_call" | custom-call | tf_op jit(solution)/shard_map/pallas_call | solution.py:684
  89.9 0.0 copy-start.1
  89.9 1.6 %copy.16 = f32[16,16,128]{2,1,0:T(8,128)} copy(f32[16,16,128]{2,1,0:T(8,128)} %get-tuple-element.6) | data formatting | bytes 262144
  91.5 0.0 copy-done.1
  91.5 0.0 copy-start
  91.5 0.6 copy.17
  92.1 0.1 copy-done
  92.2 0.6 copy.18
Async XLA Ops:
  89.9 1.6 %copy-start.1 = (f32[48,48]{1,0:T(8,128)S(1)}, f32[48,48]{1,0:T(8,128)}, u32[]{:S(2)}) copy-start(f32[48,48]{1,0:T(8,128)} %get-tuple-element.7) | copy-start | bytes 27652
  91.5 0.7 copy-start

commit v3 on v2

--- a/solution.py
+++ b/solution.py
@@ -16,7 +16,7 @@
 N = 128
 H = 32
 T = 2
-LAST = 8
+LAST = 6
 
 
 def iota(shape, dim):
@@ -79,22 +79,24 @@
     out_ref, ga_ref, gb_ref,
     x_ref, p_ref, own_ref, oth_ref, mass_ref, cols_ref, deg_ref, send_ref, pair_ref, part_ref, in_sems,
     B, D, hd, hdc, diag, v, y, e, acc, vv, w_ref, qb, gram1, gram2,
-    vcat, wcat, rr, Gl, GS, GHs, Pn, Pr, Ql, Qh, raw,
-    sndh, rcvh, sndc, rcvc, sndd, rcvd, ar_bufs,
-    hs, hr, cs, cr, ds, dr, ar_ss, ar_rs, vouched,
+    vcat, wcat, rr, Gl, GS, GHs, Pn, Pr, Ql, Qh, raw, PK, GH2, REP, BP, hdcT, TG, SEL, repv, wcat2,
+    sndh, rcvh, sndc, rcvc, sndd, rcvd, sndk, rcvk, rcvq, sndm, rcvm, ar_bufs,
+    hs, hr, cs, cr, ds, dr, ks, kr, qs, qr, ms, mr, bs, br, ts, tr, ar_ss, ar_rs, vouched,
 ):
     me = lax.axis_index("dom")
     lower = lax.rem(me + n_dom - 1, n_dom)
     upper = lax.rem(me + 1, n_dom)
+    lower2 = lax.rem(me + n_dom - 2, n_dom)
+    upper2 = lax.rem(me + 2, n_dom)
     groups = [[Groups(me, dims) for dims in stages] for stages in ar_dims]
     bar_groups = groups[1]
 
     barrier = pltpu.get_barrier_semaphore()
-    for d in (lower, upper):
+    for d in (lower, upper, lower2, upper2):
         pl.semaphore_signal(barrier, inc=1, device_id=(d,), device_id_type=MESH)
     wide, ring = bar_groups
     reach = 4
-    n_bar = 2 + wide.size - 1 + 2 * reach
+    n_bar = 4 + wide.size - 1 + 2 * reach
 
     def greet(g, t):
         pl.semaphore_signal(barrier, inc=1, device_id=(g.device(g.peer(t)),), device_id_type=MESH)
@@ -122,12 +124,16 @@
     for j in (5, 9, 7, 8, 6, 3, 2, 0, 1, 4):
         fetch(j).start()
 
-    def pair_copies(snd, rcv, ss, rs, idx):
+    def pair_copies(snd, rcv, ss, rs, idx, far_idx=None):
         out = []
-        for side, (src, dst, dev) in enumerate(((0, 16, lower), (16, 0, upper))):
+        devices = (lower, upper) if far_idx is None else (lower2, upper2)
+        src_idx = idx
+        if far_idx is not None:
+            idx = far_idx
+        for side, (src, dst, dev) in enumerate(((0, 16, devices[0]), (16, 0, devices[1]))):
             out.append(
                 pltpu.make_async_remote_copy(
-                    snd.at[idx + (pl.ds(src, 16),)],
+                    snd.at[src_idx + (pl.ds(src, 16),)],
                     rcv.at[idx + (pl.ds(dst, 16),)],
                     ss.at[idx + (side,)],
                     rs.at[idx + (side,)],
@@ -148,6 +154,14 @@
     def wait_send(*args):
         for c in pair_copies(*args):
             c.wait_send()
+
+    def both_copies(ref, ss, rs):
+        return [
+            pltpu.make_async_remote_copy(
+                ref.at[0], ref.at[at], ss.at[at], rs.at[at], device_id=(dev,), device_id_type=MESH
+            )
+            for at, dev in ((1, upper), (2, lower))
+        ]
 
     def ar_copy(slot, stage, t, receive):
         g = groups[slot][stage]
@@ -207,6 +221,7 @@
             GS[0:N, pl.ds((k * T + t) * N, N)] = hot
             GS[N : N + H, pl.ds((k * T + t) * N, N)] = halo
             GHs[pl.ds(t * H, H), at_k] = halo
+            GH2[pl.ds(t * 2 * H, H), at_k] = halo
     hot = one_hot(iota((N, N), 0) == part_ref[...]).astype(bf16)
     halo = one_hot(iota((H, N), 0) + N == part_ref[...]).astype(bf16)
     for t in range(T):
@@ -223,6 +238,11 @@
     for t in range(T):
         Pn[0, :, pl.ds(t * N, N)] = sel
         Pn[1, :, pl.ds(t * N, N)] = psel
+        for k in range(K):
+            PK[:, pl.ds((k * T + t) * N, N)] = jnp.zeros((N, N), bf16)
+            PK[pl.ds(k * H, H), pl.ds((k * T + t) * N, N)] = psel
+            near_pair = dot_nn(psel, GS[0:N, (k * T) * N : (k * T + 1) * N]).astype(bf16)
+            GH2[pl.ds(t * 2 * H + H, H), pl.ds(k * N, N)] = near_pair
         Pr[pl.ds(t * H, H), :] = sel
 
     def bcast_rows(ref, idx, r):
@@ -262,12 +282,13 @@
             rows = scatter_slot(k, rows)
         return rows
 
-    def far(near, rows, half_way=None):
+    def far(near, rows, half_way=None, table=None):
         rows = jnp.concatenate(split(rows), axis=0).T
+        table = GHs if table is None else table
         total = [jnp.zeros((C, N), f32)] * S
         for k in range(K):
             if k % 2 == 0:
-                got = dot_nn(rows, GHs[:, k * N : (k + 2) * N])
+                got = dot_nn(rows, table[:, k * N : (k + 2) * N])
             if k == 2 and half_way is not None:
                 half_way()
             part = got[:, (k % 2) * N : (k % 2 + 1) * N].reshape(S, C, N)
@@ -320,14 +341,54 @@
         for t, term in enumerate(split(value)):
             vcat[pl.ds(b * C, C), pl.ds(t * N, N)] = term
 
-    def after_a(i, ch, coarse_start):
-        first = i == 1
+    def k_finish(i, ch):
+        m = i - 3
+        wait_recv(sndh, rcvh, hs, hr, (i, ch))
+        wait_recv(sndh, rcvq, qs, qr, (i, ch), (m, ch))
+        mine, near, beyond = sndh[i, ch], rcvh[i, ch], rcvq[m, ch]
+        own_c = near * hdcT[0]
+        lower_c = jnp.concatenate([beyond[0:16], mine[0:16]], axis=0) * hdcT[1]
+        upper_c = jnp.concatenate([mine[16:32], beyond[16:32]], axis=0) * hdcT[2]
+        terms = split(jnp.concatenate([own_c, lower_c, upper_c], axis=0))
+        rep = dot_nn(jnp.concatenate(terms, axis=0).T, REP[...])
+        for j in range(3):
+            repv[j] = rep[:, j * N : (j + 1) * N].reshape(S, C, N)
+        for j in range(3):
+            for half in range(2):
+                total = [jnp.zeros((C, N), f32)] * 8
+                for a in range(S):
+                    value = repv[j, a]
+                    for b in range(8):
+                        total[b] = total[b] + bcast_rows(BP, (j, a), half * 8 + b) * value
+                for b in range(8):
+                    for t, term in enumerate(split(total[b])):
+                        wcat2[pl.ds((half * 8 + b) * C, C), pl.ds((j * T + t) * N, N)] = term
+        back = turned_rows(dot_nt(TG[...], wcat2[...]))
+        w_ref[...] = from_halo(own_c, Qh).reshape(S, C, N)
+        e[ch] = e[ch] + w_ref[...]
+        mid = own(w_ref, D)
+        for a in range(S):
+            acc[ch, a] = acc[ch, a] + mid[a] - back[a]
+        wait_recv(sndk, rcvk, ks, kr, (m, ch))
+        others = jnp.concatenate([term[H : 3 * H] for term in terms], axis=0)
+        rows = rcvk[m, ch] + dot_nn(SEL[...], others)
+        total = far(
+            vv.at[ch],
+            jnp.concatenate([rows, own_c], axis=0),
+            lambda: wait_recv(sndc, rcvc, cs, cr, (i, ch)),
+            GH2,
+        )
+        got = from_halo(rcvc[i, ch], Pr).reshape(S, C, N)
+        return [y[ch, a] - acc[ch, a] + got[a] + total[a] for a in range(S)]
+
+    def advance(i, ch, coarse_start, values, first):
         which = coarse_start.astype(jnp.int32)
         scale = jnp.where(coarse_start, 1.0, hd[...])
         keep = jnp.where(coarse_start, 0.0, 1.0)
-        for b, value in enumerate(a_finish(i - 1, ch)):
-            raw[b] = value
-            value = jnp.where(first & (ch == 0), x_ref[b], value)
+        for b, value in enumerate(values):
+            if first is not None:
+                raw[b] = value
+                value = jnp.where(first, x_ref[b], value)
             y[ch, b] = value
             value = value * scale[b : b + 1, :]
             v[ch, b] = value
@@ -335,18 +396,17 @@
             split_pair(b, value)
         send_rows(i, ch, which)
 
-    def after_q(i, ch):
-        wait_recv(sndh, rcvh, hs, hr, (i - 1, ch))
-        got = from_halo(rcvh[i - 1, ch], Qh).reshape(S, C, N)
+    def coarse_rest(i, ch):
+        m = i - 3
+        start(sndh, rcvq, qs, qr, (i, ch), (m, ch))
+        pairs = dot_nn(vcat[...], Ql[...]).reshape(S, C, N)
         for b in range(S):
-            value = (acc[ch, b] + got[b]) * hdc[b : b + 1, :]
+            value = (y[ch, b] + pairs[b]) * hdc[b : b + 1, :]
             v[ch, b] = value
             e[ch, b] = e[ch, b] + value
             split_pair(b, value)
-        send_rows(i, ch, 0)
-
-    def q_rest(ch):
-        acc[ch] = y[ch] + dot_nn(vcat[...], Ql[...]).reshape(S, C, N)
+        sndk[m, ch] = dot_nt(Pn[0], vcat[...])
+        start(sndk, rcvk, ks, kr, (m, ch))
 
     def rr_store(row, ref, sign=1.0):
         for b in range(S):
@@ -386,6 +446,23 @@
         start(sndc, rcvc, cs, cr, (LAST, 0))
 
     for k in range(K):
+        for t, term in enumerate(split(B[k].reshape(S * S, N))):
+            wcat[:, pl.ds((k * T + t) * N, N)] = term
+    BP[0] = dot_nt(wcat[...], PK[...]).reshape(S, S, N)
+    targets = dot_nt(GS[...], PK[...]) * 0.5
+    for t in range(T):
+        TG[:, pl.ds(t * N, N)] = targets[0:N].astype(bf16)
+    sndm[...] = jnp.zeros_like(sndm)
+    sndm[:, 0:N] = targets[N : N + H]
+    sndm[:, N : 2 * N] = dot_nt(sel, jnp.concatenate([psel, jnp.zeros((N - H, N), bf16)], axis=0))
+    for t in range(T):
+        for j in range(3):
+            row = iota((H, 3 * N), 0)
+            col = iota((H, 3 * N), 1)
+            hit = (lax.div(col, N) == j) & (lax.rem(col, H) == row)
+            REP[pl.ds((t * 3 + j) * H, H), :] = one_hot(hit).astype(bf16)
+
+    for k in range(K):
         for a, value in enumerate(outer(own_ref, own_ref, k)):
             D[a] = D[a] + value * live[k]
     fetch(4).wait()
@@ -404,6 +481,9 @@
     store_split_v(p_ref)
     send_rows(0, 0, 0)
     a_rest(0, 0)
+    start(sndm, rcvm, ms, mr, ())
+    for c in both_copies(BP, bs, br):
+        c.start()
     rr_store(0, x_ref)
     rr_store(16, p_ref)
 
@@ -425,24 +505,22 @@
     def event(g, _):
         i = 1 + lax.div(g, 2)
         ch = 1 - lax.rem(g, 2)
-        coarse_end = (i == 4) | (i == 6)
-        coarse_start = (i == 3) | (i == 5)
+        coarse_end = (i == 4) | (i == 5)
+        coarse_start = (i == 3) | (i == 4)
 
         @pl.when(jnp.logical_not(coarse_end))
         def _():
-            after_a(i, ch, coarse_start)
+            advance(i, ch, coarse_start, a_finish(i - 1, ch), (i == 1) & (ch == 0))
 
         @pl.when(coarse_end)
         def _():
-            after_q(i, ch)
+            advance(i, ch, coarse_start, k_finish(i - 1, ch), None)
 
         @pl.when(coarse_start)
         def _():
-            q_rest(ch)
-
-        @pl.when(jnp.logical_not(coarse_start))
-        def _():
-            a_rest(i, ch)
+            coarse_rest(i, ch)
+
+        a_rest(i, ch)
 
         @pl.when((i == 1) & (ch == 1))
         def _():
@@ -471,11 +549,33 @@
             dcat = jnp.concatenate(split(diag[...]), axis=1)
             far_diag = from_halo(rcvd[...], Qh)[0:S]
             hdc[...] = 0.5 / (diag[...] + dot_nn(dcat, Ql[...]) + far_diag)
+            for b in range(S):
+                split_pair(b, jnp.broadcast_to(hdc[b : b + 1, :], (C, N)))
+            hdcT[0] = dot_nt(Pn[1], vcat[...])
+            for c in both_copies(hdcT, ts, tr):
+                c.start()
+
+        @pl.when(late & (i == 3))
+        def _():
+            wait_recv(sndm, rcvm, ms, mr, ())
+            for c in both_copies(BP, bs, br):
+                c.wait_recv()
+            row = iota((H, N), 0)
+            for j, keep in ((1, row < 16), (2, row >= 16)):
+                there = jnp.where(keep, rcvm[:, 0:N], 0.0).astype(bf16)
+                target = dot_tn(Pr[0:H, :], there).astype(bf16)
+                for t in range(T):
+                    TG[:, pl.ds((j * T + t) * N, N)] = target
+            same = rcvm[:, N : 2 * N]
+            half = jnp.where(row < 16, same, pltpu.roll(same, H, 1))
+            SEL[...] = (half + pltpu.roll(half, 2 * H, 1)).astype(bf16)
+            for c in both_copies(hdcT, ts, tr):
+                c.wait_recv()
 
         stages = len(groups[0])
         for s in range(stages):
 
-            @pl.when(late & (i == (2 + s if s + 1 < stages else 3 + s)))
+            @pl.when(late & (i == 2 + s))
             def _(s=s):
                 total = ar_finish(0, s)
                 if s + 1 < stages:
@@ -571,11 +671,13 @@
     def drain(g, _):
         i, ch = lax.div(g, 2), lax.rem(g, 2)
         wait_send(sndh, rcvh, hs, hr, (i, ch))
-
-        @pl.when((i != 3) & (i != 5))
-        def _():
-            wait_send(sndc, rcvc, cs, cr, (i, ch))
-
+        wait_send(sndc, rcvc, cs, cr, (i, ch))
+        return 0
+
+    def drain_coarse(g, _):
+        m, ch = lax.div(g, 2), lax.rem(g, 2)
+        wait_send(sndk, rcvk, ks, kr, (m, ch))
+        wait_send(sndh, rcvq, qs, qr, (m + 3, ch), (m, ch))
         return 0
 
     ar_start(1, 1, ar_finish(1, 0))
@@ -583,6 +685,10 @@
     wait_send(sndh, rcvh, hs, hr, (LAST, 0))
     wait_send(sndc, rcvc, cs, cr, (LAST, 0))
     wait_send(sndd, rcvd, ds, dr, ())
+    lax.fori_loop(0, 4, drain_coarse, 0)
+    wait_send(sndm, rcvm, ms, mr, ())
+    for c in both_copies(BP, bs, br) + both_copies(hdcT, ts, tr):
+        c.wait_send()
     ar_start(2, 1, ar_finish(2, 0))
     for s in range(len(groups[0])):
         ar_drain(0, s)
@@ -663,12 +769,26 @@
         vm((T * N, N), bf16),
         vm((T * H, N), bf16),
         vm((S, C, N), f32),
+        vm((N, T * K * N), bf16),
+        vm((T * 2 * H, K * N), bf16),
+        vm((T * 3 * H, 3 * N), bf16),
+        vm((3, S, S, N), f32),
+        vm((3, H, S * C), f32),
+        vm((N, 3 * T * N), bf16),
+        vm((H, N), bf16),
+        vm((3, S, C, N), f32),
+        vm((S * C, 3 * T * N), bf16),
         vm((LAST + 1, 2, H, S * C), f32),
         vm((LAST + 1, 2, H, S * C), f32),
         vm((LAST + 1, 2, H, S * C), f32),
         vm((LAST + 1, 2, H, S * C), f32),
         vm((H, 128), f32),
         vm((H, 128), f32),
+        vm((2, 2, H, S * C), f32),
+        vm((2, 2, H, S * C), f32),
+        vm((2, 2, H, S * C), f32),
+        vm((H, 2 * N), f32),
+        vm((H, 2 * N), f32),
         [[vm((size(d), rows[j], 128), f32) for d in st] for j, st in enumerate(ar_dims)],
         dma((LAST + 1, 2, 2)),
         dma((LAST + 1, 2, 2)),
@@ -676,6 +796,16 @@
         dma((LAST + 1, 2, 2)),
         dma((2,)),
         dma((2,)),
+        dma((2, 2, 2)),
+        dma((2, 2, 2)),
+        dma((2, 2, 2)),
+        dma((2, 2, 2)),
+        dma((2,)),
+        dma((2,)),
+        dma((3,)),
+        dma((3,)),
+        dma((3,)),
+        dma((3,)),
         [[dma((size(d),)) for d in st] for st in ar_dims],
         [[dma((size(d),)) for d in st] for st in ar_dims],
         pltpu.SemaphoreType.REGULAR((2,)),

time: 93.1 us -> 86.3 us (0.927)
  Pallas kernels: 89.3 us -> 82.5 us
    pallas_call x1, Pallas kernels: 89.3 us -> 82.5 us  [shards(): pl.pallas_call(functools.partial(kernel, n_dom, ar_dims), out_shape=(jax....]
where the time goes in v3:
time: 86.3 us; the launch traced here: 86.1 us
  Pallas kernels  82.5 us (96%)
  local copies, waits for them, and re-layouts  2.93 us (3%)
    pallas_call x1, Pallas kernels, shards(): pl.pallas_call(functools.partial(kernel, n_dom, ar_dims), out_shape=(jax....  82.5 us
    unnamed x7, local copies, waits for them, and re-layouts  2.93 us

profile of v3, /device:TPU:1, one launch (start us, length us, event | category | flops | bytes accessed | tf_op | source)
XLA Modules:
  0.0 86.1 jit_solution(4494948256507207627)
XLA Ops:
  0.6 82.5 %shard_map.121 = (f32[16,16,128]{2,1,0:T(8,128)}, f32[48,48]{1,0:T(8,128)}, f32[48,48]{1,0:T(8,128)}) custom-call(f32[16,16,128]{2,1,0:T(8,128)} %x_in.1, f32[16,16,128]{2,1,0:T(8,128)} %p_in.1, f32[4,16,16,128]{3,2,1,0:T(8,128)} %own_in.1, f32[4,16,16,128]{3,2,1,0:T(8,128)} %oth_in.1, f32[16,128]{1,0:T(8,128)} %mass_in.1, s32[4,128]{1,0:T(4,128)} %cols_in.1, ...), custom_call_target="tpu_custom_call" | custom-call | tf_op jit(solution)/shard_map/pallas_call | solution.py:814
  83.1 0.0 copy-start.1
  83.1 1.6 %copy.16 = f32[16,16,128]{2,1,0:T(8,128)} copy(f32[16,16,128]{2,1,0:T(8,128)} %get-tuple-element.6) | data formatting | bytes 262144
  84.7 0.0 copy-done.1
  84.7 0.0 copy-start
  84.7 0.6 copy.17
  85.3 0.1 copy-done
  85.5 0.6 copy.18
Async XLA Ops:
  83.1 1.6 %copy-start.1 = (f32[48,48]{1,0:T(8,128)S(1)}, f32[48,48]{1,0:T(8,128)}, u32[]{:S(2)}) copy-start(f32[48,48]{1,0:T(8,128)} %get-tuple-element.7) | copy-start | bytes 27652
  84.7 0.7 copy-start

commit v4 on v3

--- a/solution.py
+++ b/solution.py
@@ -79,7 +79,7 @@
     out_ref, ga_ref, gb_ref,
     x_ref, p_ref, own_ref, oth_ref, mass_ref, cols_ref, deg_ref, send_ref, pair_ref, part_ref, in_sems,
     B, D, hd, hdc, diag, v, y, e, acc, vv, w_ref, qb, gram1, gram2,
-    vcat, wcat, rr, Gl, GS, GHs, Pn, Pr, Ql, Qh, raw, PK, GH2, REP, BP, hdcT, TG, SEL, repv, wcat2,
+    vcat, wcat, rr, Gl, GS, GHs, Pn, Pr, Ql, Qh, raw, PK, GH2, REP, BP, hdcT, TG, SEL, repv, wcat2, zcat,
     sndh, rcvh, sndc, rcvc, sndd, rcvd, sndk, rcvk, rcvq, sndm, rcvm, ar_bufs,
     hs, hr, cs, cr, ds, dr, ks, kr, qs, qr, ms, mr, bs, br, ts, tr, ar_ss, ar_rs, vouched,
 ):
@@ -181,6 +181,11 @@
         g = groups[slot][stage]
         ar_bufs[slot][stage][g.pos] = value
 
+        if slot == 2:
+            for t in range(1, g.size):
+                ar_copy(slot, stage, t, False).start()
+            return
+
         def go(t, _):
             ar_copy(slot, stage, t, False).start()
             return 0
@@ -194,7 +199,11 @@
             ar_copy(slot, stage, t, True).wait_recv()
             return 0
 
-        lax.fori_loop(1, g.size, go, 0)
+        if slot == 2:
+            for t in range(1, g.size):
+                go(t, 0)
+        else:
+            lax.fori_loop(1, g.size, go, 0)
         buf = ar_bufs[slot][stage]
         total = buf[0]
         for j in range(1, g.size):
@@ -222,28 +231,14 @@
             GS[N : N + H, pl.ds((k * T + t) * N, N)] = halo
             GHs[pl.ds(t * H, H), at_k] = halo
             GH2[pl.ds(t * 2 * H, H), at_k] = halo
-    hot = one_hot(iota((N, N), 0) == part_ref[...]).astype(bf16)
-    halo = one_hot(iota((H, N), 0) + N == part_ref[...]).astype(bf16)
-    for t in range(T):
-        Ql[pl.ds(t * N, N), :] = hot
-        Qh[pl.ds(t * H, H), :] = halo
-
     def column(ref):
         square = jnp.where(iota((H, H), 0) == iota((H, H), 1), ref[...].astype(f32), 0.0)
         return jnp.sum(square, axis=1, keepdims=True)
 
     lanes = iota((H, N), 1).astype(f32)
     sel = one_hot(lanes == column(send_ref)).astype(bf16)
-    psel = one_hot(lanes == column(pair_ref)).astype(bf16)
     for t in range(T):
         Pn[0, :, pl.ds(t * N, N)] = sel
-        Pn[1, :, pl.ds(t * N, N)] = psel
-        for k in range(K):
-            PK[:, pl.ds((k * T + t) * N, N)] = jnp.zeros((N, N), bf16)
-            PK[pl.ds(k * H, H), pl.ds((k * T + t) * N, N)] = psel
-            near_pair = dot_nn(psel, GS[0:N, (k * T) * N : (k * T + 1) * N]).astype(bf16)
-            GH2[pl.ds(t * 2 * H + H, H), pl.ds(k * N, N)] = near_pair
-        Pr[pl.ds(t * H, H), :] = sel
 
     def bcast_rows(ref, idx, r):
         return ref[idx + (slice(r, r + 1), slice(None))]
@@ -289,7 +284,7 @@
         for k in range(K):
             if k % 2 == 0:
                 got = dot_nn(rows, table[:, k * N : (k + 2) * N])
-            if k == 2 and half_way is not None:
+            if k == 3 and half_way is not None:
                 half_way()
             part = got[:, (k % 2) * N : (k % 2 + 1) * N].reshape(S, C, N)
             near[k] = near[k] + part
@@ -316,13 +311,15 @@
         sndh[i, ch] = dot_nt(Pn[which], vcat[...])
         start(sndh, rcvh, hs, hr, (i, ch))
 
-    def a_rest(i, ch, enter=None):
+    def a_rest(i, ch):
         src = v.at[ch]
         rows = reverse(src)
         sndc[i, ch] = rows[N : N + H]
-        if enter is not None:
-            enter()
         start(sndc, rcvc, cs, cr, (i, ch))
+        a_local(ch, rows)
+
+    def a_local(ch, rows):
+        src = v.at[ch]
         gather_local(vv.at[ch])
         back = turned_rows(rows)
         total = own(src, D)
@@ -413,6 +410,38 @@
             for t, term in enumerate(split(sign * ref[b])):
                 rr[pl.ds(t * 128 + row, C), pl.ds(b * N, N)] = term
 
+    def later_tables():
+        hot = one_hot(iota((N, N), 0) == part_ref[...]).astype(bf16)
+        halo = one_hot(iota((H, N), 0) + N == part_ref[...]).astype(bf16)
+        for t in range(T):
+            Ql[pl.ds(t * N, N), :] = hot
+            Qh[pl.ds(t * H, H), :] = halo
+        psel = one_hot(lanes == column(pair_ref)).astype(bf16)
+        for t in range(T):
+            Pn[1, :, pl.ds(t * N, N)] = psel
+            for k in range(K):
+                PK[:, pl.ds((k * T + t) * N, N)] = jnp.zeros((N, N), bf16)
+                PK[pl.ds(k * H, H), pl.ds((k * T + t) * N, N)] = psel
+                near_pair = dot_nn(psel, GS[0:N, (k * T) * N : (k * T + 1) * N]).astype(bf16)
+                GH2[pl.ds(t * 2 * H + H, H), pl.ds(k * N, N)] = near_pair
+            Pr[pl.ds(t * H, H), :] = sel
+        for k in range(K):
+            for t, term in enumerate(split(B[k].reshape(S * S, N))):
+                wcat[:, pl.ds((k * T + t) * N, N)] = term
+        BP[0] = dot_nt(wcat[...], PK[...]).reshape(S, S, N)
+        targets = dot_nt(GS[...], PK[...]) * 0.5
+        for t in range(T):
+            TG[:, pl.ds(t * N, N)] = targets[0:N].astype(bf16)
+        sndm[...] = jnp.zeros_like(sndm)
+        sndm[:, 0:N] = targets[N : N + H]
+        sndm[:, N : 2 * N] = dot_nt(sel, jnp.concatenate([psel, jnp.zeros((N - H, N), bf16)], axis=0))
+        for t in range(T):
+            for j in range(3):
+                row = iota((H, 3 * N), 0)
+                col = iota((H, 3 * N), 1)
+                hit = (lax.div(col, N) == j) & (lax.rem(col, H) == row)
+                REP[pl.ds((t * 3 + j) * H, H), :] = one_hot(hit).astype(bf16)
+
     live = [jnp.where(deg_ref[...] > k, 1.0, 0.0).astype(f32) for k in range(K)]
 
     def outer(left, right, k):
@@ -422,9 +451,6 @@
 
         return lax.fori_loop(0, S, body, tuple(jnp.zeros((S, N), f32) for _ in range(S)), unroll=4)
 
-    rr[...] = jnp.zeros_like(rr)
-    e[...] = jnp.zeros_like(e)
-    y[...] = jnp.zeros_like(y)
     fetch(3).wait()
     rows = None
     for k in range(K):
@@ -439,53 +465,36 @@
             B[k, a] = value * live[k]
     fetch(0).wait()
     v[1] = x_ref[...]
-
-    def enter():
-        pl.semaphore_wait(barrier, n_bar)
-        vouch()
-        start(sndc, rcvc, cs, cr, (LAST, 0))
-
-    for k in range(K):
-        for t, term in enumerate(split(B[k].reshape(S * S, N))):
-            wcat[:, pl.ds((k * T + t) * N, N)] = term
-    BP[0] = dot_nt(wcat[...], PK[...]).reshape(S, S, N)
-    targets = dot_nt(GS[...], PK[...]) * 0.5
-    for t in range(T):
-        TG[:, pl.ds(t * N, N)] = targets[0:N].astype(bf16)
-    sndm[...] = jnp.zeros_like(sndm)
-    sndm[:, 0:N] = targets[N : N + H]
-    sndm[:, N : 2 * N] = dot_nt(sel, jnp.concatenate([psel, jnp.zeros((N - H, N), bf16)], axis=0))
-    for t in range(T):
-        for j in range(3):
-            row = iota((H, 3 * N), 0)
-            col = iota((H, 3 * N), 1)
-            hit = (lax.div(col, N) == j) & (lax.rem(col, H) == row)
-            REP[pl.ds((t * 3 + j) * H, H), :] = one_hot(hit).astype(bf16)
-
+    store_split_v(x_ref)
+    sndh[0, 1] = dot_nt(Pn[0], vcat[...])
+    rows = reverse(v.at[1])
+    sndc[0, 1] = rows[N : N + H]
+    pl.semaphore_wait(barrier, n_bar)
+    vouch()
+    start(sndh, rcvh, hs, hr, (0, 1))
+    start(sndc, rcvc, cs, cr, (LAST, 0))
+    start(sndc, rcvc, cs, cr, (0, 1))
     for k in range(K):
         for a, value in enumerate(outer(own_ref, own_ref, k)):
             D[a] = D[a] + value * live[k]
     fetch(4).wait()
     for b in range(S):
         D[b, b : b + 1, :] = D[b, b : b + 1, :] + mass_ref[b : b + 1, :]
-    store_split_v(x_ref)
-    sndh[0, 1] = dot_nt(Pn[0], vcat[...])
-
-    def enter_and_send():
-        enter()
-        start(sndh, rcvh, hs, hr, (0, 1))
-
-    a_rest(0, 1, enter_and_send)
+    a_local(1, rows)
     fetch(1).wait()
     v[0] = p_ref[...]
     store_split_v(p_ref)
     send_rows(0, 0, 0)
     a_rest(0, 0)
+    e[...] = jnp.zeros_like(e)
+    y[...] = jnp.zeros_like(y)
+    rr[...] = jnp.zeros_like(rr)
+    rr_store(0, x_ref)
+    rr_store(16, p_ref)
+    later_tables()
     start(sndm, rcvm, ms, mr, ())
     for c in both_copies(BP, bs, br):
         c.start()
-    rr_store(0, x_ref)
-    rr_store(16, p_ref)
 
     wait_recv(sndc, rcvc, cs, cr, (LAST, 0))
     w_ref[...] = from_halo(rcvc[LAST, 0], Pr).reshape(S, S, N)
@@ -652,21 +661,29 @@
         return jnp.where(lane < 16, pltpu.roll(value, 128 - source, 1), 0.0)
 
     gram2[0:2, :] = pack_block(lanes_from(parts, 64))
+    rows = reverse(w_ref)
+    turned = jnp.concatenate([term[0 : 2 * H] for term in split(jnp.concatenate([rows[N : N + H], rows[N : N + H]], axis=0))], axis=0).T
+    zcat[...] = turned
     gather_local(vv.at[0])
-    total = own(w_ref, D)
+    back = turned_rows(rows)
+    near = vv.at[0]
+    mid = own(w_ref, D)
     for a in range(S):
-        acc[0, a] = 0.5 * total[a]
+        acc[0, a] = mid[a] - back[a]
+    mid = far(near, jnp.zeros((H, S * C), f32))
+    for a in range(S):
+        v[0, a] = acc[0, a] - mid[a]
+    rr_store(80, v.at[0])
+    parts = dot_nt(left, rr[...])
+    parts = parts[0:16, 0:128] + parts[0:16, 128:256] + parts[16:32, 0:128] + parts[16:32, 128:256]
+    gram2[2:4, :] = pack_block(lanes_from(parts, 80) * scale)
     wait_recv(sndh, rcvh, hs, hr, (LAST, 0))
-    total = far(vv.at[0], rcvh[LAST, 0])
-    for a in range(S):
-        v[0, a] = acc[0, a] - total[a]
-    rr_store(80, v.at[0])
-    images = jnp.concatenate([rr[80:96, :], rr[208:224, :]], axis=0)
-    left = jnp.concatenate([rr[64:80, :], rr[192:208, :]], axis=0)
-    parts = dot_nt(jnp.concatenate([left, images], axis=0), rr[...])
-    parts = parts[:, 0:128] + parts[:, 128:256]
-    both = lanes_from(parts[0:16] + parts[16:32], 80) + lanes_from(parts[32:48] + parts[48:64], 64)
-    ar_start(2, 0, jnp.concatenate([pack_block(both * scale), gram2[0:2, :]], axis=0))
+    terms = split(rcvh[LAST, 0])
+    edges = dot_nn(zcat[...], jnp.concatenate([terms[0], terms[1], terms[0], terms[1]], axis=0))
+    same = lax.div(iota((S * C, S * C), 0), C) == lax.div(iota((S * C, S * C), 1), C)
+    edges = jnp.sum(jnp.where(same, edges, 0.0).reshape(S, C, S * C), axis=0)
+    edges = edges[:, 0:128] + edges[:, 128:256]
+    ar_start(2, 0, jnp.concatenate([gram2[2:4, :] - pack_block(edges * (2.0 * scale)), gram2[0:2, :]], axis=0))
 
     def drain(g, _):
         i, ch = lax.div(g, 2), lax.rem(g, 2)
@@ -714,10 +731,22 @@
     wide_b = place(g2, 0, 0) + place(g2, 16, 32)
     ar_drain(1, 1)
     last = ar_finish(2, 1)
-    ga_ref[16:32, :] = (wide_a + place(unpack_block(last[0:2]), 16, 16))[:, 0:48]
+    image = unpack_block(last[0:2])
+    square = jnp.concatenate([jnp.where(lane < 16, image, 0.0), jnp.zeros((128 - C, 128), f32)], axis=0).T
+    image = 0.5 * (jnp.where(lane < 16, image, 0.0) + square[0:16, :])
+    ga_ref[16:32, :] = (wide_a + place(image, 0, 16))[:, 0:48]
     gb_ref[16:32, :] = (wide_b + place(unpack_block(last[2:4]), 16, 16))[:, 0:48]
     ar_drain(2, 1)
     result.wait()
+
+
+def move_results(a_in, b_in, c_in, a_out, b_out, c_out, sems):
+    pairs = ((a_in, a_out), (b_in, b_out), (c_in, c_out))
+    copies = [pltpu.make_async_copy(src, dst, sems.at[j]) for j, (src, dst) in enumerate(pairs)]
+    for c in copies:
+        c.start()
+    for c in copies:
+        c.wait()
 
 
 def shards(n_dom, ar_dims, x, p, f_own, f_other, mass, cols, degree, send, pair, partner):
@@ -778,6 +807,7 @@
         vm((H, N), bf16),
         vm((3, S, C, N), f32),
         vm((S * C, 3 * T * N), bf16),
+        vm((S * C, 2 * T * H), bf16),
         vm((LAST + 1, 2, H, S * C), f32),
         vm((LAST + 1, 2, H, S * C), f32),
         vm((LAST + 1, 2, H, S * C), f32),
@@ -811,7 +841,7 @@
         pltpu.SemaphoreType.REGULAR((2,)),
     ]
     whole = pl.BlockSpec(memory_space=pltpu.VMEM)
-    return pl.pallas_call(
+    results = pl.pallas_call(
         functools.partial(kernel, n_dom, ar_dims),
         out_shape=(
             jax.ShapeDtypeStruct((S, C, N), f32),
@@ -828,6 +858,14 @@
         x, p, f_own, f_other, mass, cols,
         degree.reshape(1, N), send.reshape(1, H), pair.reshape(1, H), partner.reshape(1, N),
     )
+    any_space = pl.BlockSpec(memory_space=pl.ANY)
+    return pl.pallas_call(
+        move_results,
+        out_shape=tuple(jax.ShapeDtypeStruct(r.shape, r.dtype) for r in results),
+        in_specs=[any_space] * 3,
+        out_specs=(any_space,) * 3,
+        scratch_shapes=[dma((3,))],
+    )(*results)
 
 
 def solution(mesh):

time: 86.3 us -> 87.2 us (1.010)
  Pallas kernels: 82.5 us -> 86.4 us
  local copies, waits for them, and re-layouts: 2.93 us -> 0 us
    pallas_call x0 -> x1, Pallas kernels: none -> 6.59 us  [shards(): pl.pallas_call(move_results, out_shape=tuple((jax.ShapeDtypeStruct(r.shap...]
    unnamed x7 -> x0, local copies, waits for them, and re-layouts: 2.93 us -> none
    pallas_call x1, Pallas kernels: 82.5 us -> 79.8 us  [shards(): pl.pallas_call(functools.partial(kernel, n_dom, ar_dims), out_shape=(jax....]
where the time goes in v4:
time: 87.2 us; the launch traced here: 87 us
  Pallas kernels  86.4 us (99%)
    pallas_call x1, Pallas kernels, shards(): pl.pallas_call(functools.partial(kernel, n_dom, ar_dims), out_shape=(jax....  79.8 us
    pallas_call x1, Pallas kernels, shards(): pl.pallas_call(move_results, out_shape=tuple((jax.ShapeDtypeStruct(r.shap...  6.59 us

profile of v4, /device:TPU:1, one launch (start us, length us, event | category | flops | bytes accessed | tf_op | source)
XLA Modules:
  0.0 87.0 jit_solution(12291331219568348103)
XLA Ops:
  0.6 79.8 %shard_map.121 = (f32[16,16,128]{2,1,0:T(8,128)}, f32[48,48]{1,0:T(8,128)}, f32[48,48]{1,0:T(8,128)}) custom-call(f32[16,16,128]{2,1,0:T(8,128)} %x_in.1, f32[16,16,128]{2,1,0:T(8,128)} %p_in.1, f32[4,16,16,128]{3,2,1,0:T(8,128)} %own_in.1, f32[4,16,16,128]{3,2,1,0:T(8,128)} %oth_in.1, f32[16,128]{1,0:T(8,128)} %mass_in.1, s32[4,128]{1,0:T(4,128)} %cols_in.1, ...), custom_call_target="tpu_custom_call" | custom-call | tf_op jit(solution)/shard_map/pallas_call | solution.py:844
  80.5 6.6 %shard_map.122 = (f32[16,16,128]{2,1,0:T(8,128)}, f32[48,48]{1,0:T(8,128)}, f32[48,48]{1,0:T(8,128)}) custom-call(f32[16,16,128]{2,1,0:T(8,128)} %get-tuple-element.6.a_in, f32[48,48]{1,0:T(8,128)} %get-tuple-element.7.b_in, f32[48,48]{1,0:T(8,128)} %get-tuple-element.8.c_in), custom_call_target="tpu_custom_call" | custom-call | tf_op jit(solution)/shard_map/pallas_call | solution.py:862

commit v5 on v4

--- a/solution.py
+++ b/solution.py
@@ -609,7 +609,7 @@
     lax.fori_loop(0, 2 * (LAST - 1), event, 0)
 
     def last_event(g, _):
-        ch = g
+        ch = 1 - g
         for b, value in enumerate(a_finish(LAST - 1, ch)):
             e[ch, b] = e[ch, b] + value * hd[b : b + 1, :]
         return 0
@@ -740,12 +740,16 @@
     result.wait()
 
 
-def move_results(a_in, b_in, c_in, a_out, b_out, c_out, sems):
-    pairs = ((a_in, a_out), (b_in, b_out), (c_in, c_out))
-    copies = [pltpu.make_async_copy(src, dst, sems.at[j]) for j, (src, dst) in enumerate(pairs)]
-    for c in copies:
+def move_results(a_in, b_in, c_in, a_out, b_out, c_out, a_mid, b_mid, c_mid, sems):
+    sets = ((a_in, a_mid, a_out), (b_in, b_mid, b_out), (c_in, c_mid, c_out))
+    first = [pltpu.make_async_copy(src, mid, sems.at[j]) for j, (src, mid, _) in enumerate(sets)]
+    second = [pltpu.make_async_copy(mid, dst, sems.at[3 + j]) for j, (_, mid, dst) in enumerate(sets)]
+    for c in first:
         c.start()
-    for c in copies:
+    for before, after in zip(first, second):
+        before.wait()
+        after.start()
+    for c in second:
         c.wait()
 
 
@@ -864,7 +868,7 @@
         out_shape=tuple(jax.ShapeDtypeStruct(r.shape, r.dtype) for r in results),
         in_specs=[any_space] * 3,
         out_specs=(any_space,) * 3,
-        scratch_shapes=[dma((3,))],
+        scratch_shapes=[vm(r.shape, r.dtype) for r in results] + [dma((6,))],
     )(*results)
 
 

time: 87.2 us -> 81.9 us (0.939)
  Pallas kernels: 86.4 us -> 81.1 us
    pallas_call x1, Pallas kernels: 6.59 us -> 1.62 us  [shards(): pl.pallas_call(move_results, out_shape=tuple((jax.ShapeDtypeStruct(r.shap...]
where the time goes in v5:
time: 81.9 us; the launch traced here: 81.8 us
  Pallas kernels  81.1 us (99%)
    pallas_call x1, Pallas kernels, shards(): pl.pallas_call(functools.partial(kernel, n_dom, ar_dims), out_shape=(jax....  79.5 us

profile of v5, /device:TPU:1, one launch (start us, length us, event | category | flops | bytes accessed | tf_op | source)
XLA Modules:
  0.0 81.8 jit_solution(16320942057272974476)
XLA Ops:
  0.6 79.5 %shard_map.121 = (f32[16,16,128]{2,1,0:T(8,128)}, f32[48,48]{1,0:T(8,128)}, f32[48,48]{1,0:T(8,128)}) custom-call(f32[16,16,128]{2,1,0:T(8,128)} %x_in.1, f32[16,16,128]{2,1,0:T(8,128)} %p_in.1, f32[4,16,16,128]{3,2,1,0:T(8,128)} %own_in.1, f32[4,16,16,128]{3,2,1,0:T(8,128)} %oth_in.1, f32[16,128]{1,0:T(8,128)} %mass_in.1, s32[4,128]{1,0:T(4,128)} %cols_in.1, ...), custom_call_target="tpu_custom_call" | custom-call | tf_op jit(solution)/shard_map/pallas_call | solution.py:848
  80.2 1.6 %shard_map.122 = (f32[16,16,128]{2,1,0:T(8,128)}, f32[48,48]{1,0:T(8,128)}, f32[48,48]{1,0:T(8,128)}) custom-call(f32[16,16,128]{2,1,0:T(8,128)} %get-tuple-element.6.a_in, f32[48,48]{1,0:T(8,128)} %get-tuple-element.7.b_in, f32[48,48]{1,0:T(8,128)} %get-tuple-element.8.c_in), custom_call_target="tpu_custom_call" | custom-call | tf_op jit(solution)/shard_map/pallas_call | solution.py:866

commit v6 on v5

--- a/solution.py
+++ b/solution.py
@@ -79,7 +79,7 @@
     out_ref, ga_ref, gb_ref,
     x_ref, p_ref, own_ref, oth_ref, mass_ref, cols_ref, deg_ref, send_ref, pair_ref, part_ref, in_sems,
     B, D, hd, hdc, diag, v, y, e, acc, vv, w_ref, qb, gram1, gram2,
-    vcat, wcat, rr, Gl, GS, GHs, Pn, Pr, Ql, Qh, raw, PK, GH2, REP, BP, hdcT, TG, SEL, repv, wcat2, zcat,
+    vcat, wcat, rr, Gl, GS, GHs, Pn, Pr, Ql, Qh, raw, PK, GH2, REP, BP, hdcT, TG, SEL, repv, wcat2, zcat, back_rows,
     sndh, rcvh, sndc, rcvc, sndd, rcvd, sndk, rcvk, rcvq, sndm, rcvm, ar_bufs,
     hs, hr, cs, cr, ds, dr, ks, kr, qs, qr, ms, mr, bs, br, ts, tr, ar_ss, ar_rs, vouched,
 ):
@@ -247,10 +247,10 @@
         for t, term in enumerate(split(value)):
             wcat[pl.ds(b * C, C), pl.ds((k * T + t) * N, N)] = term
 
-    def store_split_v(ref):
+    def store_split_v(ref, cur=0):
         for b in range(S):
             for t, term in enumerate(split(ref[b])):
-                vcat[pl.ds(b * C, C), pl.ds(t * N, N)] = term
+                vcat[cur, pl.ds(b * C, C), pl.ds(t * N, N)] = term
 
     def scatter_slot(k, total):
         at_k = slice(k * T * N, (k + 1) * T * N)
@@ -302,25 +302,26 @@
                 total[a] = total[a] + bcast_rows(D, (a,), b) * value
         return total
 
-    def gather_local(dst):
-        rows = dot_nn(vcat[...], Gl[...])
+    def gather_local(dst, cur=0):
+        rows = dot_nn(vcat[cur], Gl[...])
         for k in range(K):
             dst[k] = rows[:, k * N : (k + 1) * N].reshape(S, C, N)
 
     def send_rows(i, ch, which):
-        sndh[i, ch] = dot_nt(Pn[which], vcat[...])
+        cur = ch
+        sndh[i, ch] = dot_nt(Pn[which], vcat[cur])
         start(sndh, rcvh, hs, hr, (i, ch))
 
-    def a_rest(i, ch):
-        src = v.at[ch]
-        rows = reverse(src)
+    def a_send(i, ch):
+        rows = reverse(v.at[ch])
         sndc[i, ch] = rows[N : N + H]
         start(sndc, rcvc, cs, cr, (i, ch))
-        a_local(ch, rows)
-
-    def a_local(ch, rows):
+        back_rows[ch] = rows[0:N]
+
+    def a_local(ch):
         src = v.at[ch]
-        gather_local(vv.at[ch])
+        rows = back_rows[ch]
+        gather_local(vv.at[ch], ch)
         back = turned_rows(rows)
         total = own(src, D)
         for a in range(S):
@@ -334,14 +335,15 @@
         got = from_halo(rcvc[i, ch], Pr).reshape(S, C, N)
         return [y[ch, a] - acc[ch, a] + got[a] + total[a] for a in range(S)]
 
-    def split_pair(b, value):
+    def split_pair(b, value, cur):
         for t, term in enumerate(split(value)):
-            vcat[pl.ds(b * C, C), pl.ds(t * N, N)] = term
+            vcat[cur, pl.ds(b * C, C), pl.ds(t * N, N)] = term
 
     def k_finish(i, ch):
         m = i - 3
         wait_recv(sndh, rcvh, hs, hr, (i, ch))
         wait_recv(sndh, rcvq, qs, qr, (i, ch), (m, ch))
+        wait_recv(sndk, rcvk, ks, kr, (m, ch))
         mine, near, beyond = sndh[i, ch], rcvh[i, ch], rcvq[m, ch]
         own_c = near * hdcT[0]
         lower_c = jnp.concatenate([beyond[0:16], mine[0:16]], axis=0) * hdcT[1]
@@ -366,7 +368,6 @@
         mid = own(w_ref, D)
         for a in range(S):
             acc[ch, a] = acc[ch, a] + mid[a] - back[a]
-        wait_recv(sndk, rcvk, ks, kr, (m, ch))
         others = jnp.concatenate([term[H : 3 * H] for term in terms], axis=0)
         rows = rcvk[m, ch] + dot_nn(SEL[...], others)
         total = far(
@@ -390,19 +391,20 @@
             value = value * scale[b : b + 1, :]
             v[ch, b] = value
             e[ch, b] = e[ch, b] + keep * value
-            split_pair(b, value)
+            split_pair(b, value, ch)
         send_rows(i, ch, which)
 
     def coarse_rest(i, ch):
         m = i - 3
+        cur = ch
         start(sndh, rcvq, qs, qr, (i, ch), (m, ch))
-        pairs = dot_nn(vcat[...], Ql[...]).reshape(S, C, N)
+        pairs = dot_nn(vcat[cur], Ql[...]).reshape(S, C, N)
         for b in range(S):
             value = (y[ch, b] + pairs[b]) * hdc[b : b + 1, :]
             v[ch, b] = value
             e[ch, b] = e[ch, b] + value
-            split_pair(b, value)
-        sndk[m, ch] = dot_nt(Pn[0], vcat[...])
+            split_pair(b, value, ch)
+        sndk[m, ch] = dot_nt(Pn[0], vcat[cur])
         start(sndk, rcvk, ks, kr, (m, ch))
 
     def rr_store(row, ref, sign=1.0):
@@ -465,10 +467,11 @@
             B[k, a] = value * live[k]
     fetch(0).wait()
     v[1] = x_ref[...]
-    store_split_v(x_ref)
-    sndh[0, 1] = dot_nt(Pn[0], vcat[...])
+    store_split_v(x_ref, 1)
+    sndh[0, 1] = dot_nt(Pn[0], vcat[1])
     rows = reverse(v.at[1])
     sndc[0, 1] = rows[N : N + H]
+    back_rows[1] = rows[0:N]
     pl.semaphore_wait(barrier, n_bar)
     vouch()
     start(sndh, rcvh, hs, hr, (0, 1))
@@ -480,12 +483,13 @@
     fetch(4).wait()
     for b in range(S):
         D[b, b : b + 1, :] = D[b, b : b + 1, :] + mass_ref[b : b + 1, :]
-    a_local(1, rows)
+    a_local(1)
     fetch(1).wait()
     v[0] = p_ref[...]
     store_split_v(p_ref)
     send_rows(0, 0, 0)
-    a_rest(0, 0)
+    a_send(0, 0)
+    a_local(0)
     e[...] = jnp.zeros_like(e)
     y[...] = jnp.zeros_like(y)
     rr[...] = jnp.zeros_like(rr)
@@ -511,9 +515,8 @@
     sndd[:, 0:S] = dot_nt(Pn[1], dcat)
     start(sndd, rcvd, ds, dr, ())
 
-    def event(g, _):
-        i = 1 + lax.div(g, 2)
-        ch = 1 - lax.rem(g, 2)
+    def event(i, g):
+        ch = 1 - g
         coarse_end = (i == 4) | (i == 5)
         coarse_start = (i == 3) | (i == 4)
 
@@ -529,17 +532,25 @@
         def _():
             coarse_rest(i, ch)
 
-        a_rest(i, ch)
-
-        @pl.when((i == 1) & (ch == 1))
+        a_send(i, ch)
+        return 0
+
+    def both_chains(j, _):
+        i = 1 + j
+        lax.fori_loop(0, 2, lambda g, c: event(i, g), 0)
+
+        @pl.when(i == 1)
         def _():
-            rr_store(32, raw, -1.0)
-
-        @pl.when((i == 1) & (ch == 0))
-        def _():
+            rr_store(32, y.at[1], -1.0)
             rr_store(48, raw, -1.0)
 
-        late = ch == 0
+        def rest(g, _):
+            a_local(1 - g)
+            return 0
+
+        lax.fori_loop(0, 2, rest, 0)
+        late = i > 0
+
 
         @pl.when(late & (i == 1))
         def _():
@@ -559,8 +570,8 @@
             far_diag = from_halo(rcvd[...], Qh)[0:S]
             hdc[...] = 0.5 / (diag[...] + dot_nn(dcat, Ql[...]) + far_diag)
             for b in range(S):
-                split_pair(b, jnp.broadcast_to(hdc[b : b + 1, :], (C, N)))
-            hdcT[0] = dot_nt(Pn[1], vcat[...])
+                split_pair(b, jnp.broadcast_to(hdc[b : b + 1, :], (C, N)), 0)
+            hdcT[0] = dot_nt(Pn[1], vcat[0])
             for c in both_copies(hdcT, ts, tr):
                 c.start()
 
@@ -606,7 +617,7 @@
 
         return 0
 
-    lax.fori_loop(0, 2 * (LAST - 1), event, 0)
+    lax.fori_loop(0, LAST - 1, both_chains, 0)
 
     def last_event(g, _):
         ch = 1 - g
@@ -628,7 +639,7 @@
     result = pltpu.make_async_copy(w_ref, out_ref, in_sems.at[10])
     result.start()
     store_split_v(w_ref)
-    sndh[LAST, 0] = dot_nt(Pn[0], vcat[...])
+    sndh[LAST, 0] = dot_nt(Pn[0], vcat[0])
     start(sndh, rcvh, hs, hr, (LAST, 0))
     rr_store(64, w_ref)
     lane = iota((C, 128), 1)
@@ -702,11 +713,11 @@
     wait_send(sndh, rcvh, hs, hr, (LAST, 0))
     wait_send(sndc, rcvc, cs, cr, (LAST, 0))
     wait_send(sndd, rcvd, ds, dr, ())
+    ar_start(2, 1, ar_finish(2, 0))
     lax.fori_loop(0, 4, drain_coarse, 0)
     wait_send(sndm, rcvm, ms, mr, ())
     for c in both_copies(BP, bs, br) + both_copies(hdcT, ts, tr):
         c.wait_send()
-    ar_start(2, 1, ar_finish(2, 0))
     for s in range(len(groups[0])):
         ar_drain(0, s)
     ar_drain(1, 0)
@@ -791,7 +802,7 @@
         vm((C, C, 128), f32),
         vm((C, 128), f32),
         vm((C, 128), f32),
-        vm((S * C, T * N), bf16),
+        vm((2, S * C, T * N), bf16),
         vm((S * C, T * K * N), bf16),
         vm((256, S * N), bf16),
         vm((T * N, K * N), bf16),
@@ -812,6 +823,7 @@
         vm((3, S, C, N), f32),
         vm((S * C, 3 * T * N), bf16),
         vm((S * C, 2 * T * H), bf16),
+        vm((2, N, S * C), f32),
         vm((LAST + 1, 2, H, S * C), f32),
         vm((LAST + 1, 2, H, S * C), f32),
         vm((LAST + 1, 2, H, S * C), f32),

time: 81.9 us -> 81.1 us (level)
  no operation moved by 1% of the time
where the time goes in v6:
time: 81.1 us; the launch traced here: 81 us
  Pallas kernels  80.3 us (99%)
    pallas_call x1, Pallas kernels, shards(): pl.pallas_call(functools.partial(kernel, n_dom, ar_dims), out_shape=(jax....  78.7 us

profile of v6, /device:TPU:1, one launch (start us, length us, event | category | flops | bytes accessed | tf_op | source)
XLA Modules:
  0.0 81.0 jit_solution(15265925249810146250)
XLA Ops:
  0.6 78.7 %shard_map.121 = (f32[16,16,128]{2,1,0:T(8,128)}, f32[48,48]{1,0:T(8,128)}, f32[48,48]{1,0:T(8,128)}) custom-call(f32[16,16,128]{2,1,0:T(8,128)} %x_in.1, f32[16,16,128]{2,1,0:T(8,128)} %p_in.1, f32[4,16,16,128]{3,2,1,0:T(8,128)} %own_in.1, f32[4,16,16,128]{3,2,1,0:T(8,128)} %oth_in.1, f32[16,128]{1,0:T(8,128)} %mass_in.1, s32[4,128]{1,0:T(4,128)} %cols_in.1, ...), custom_call_target="tpu_custom_call" | custom-call | tf_op jit(solution)/shard_map/pallas_call | solution.py:860
  79.4 1.6 %shard_map.122 = (f32[16,16,128]{2,1,0:T(8,128)}, f32[48,48]{1,0:T(8,128)}, f32[48,48]{1,0:T(8,128)}) custom-call(f32[16,16,128]{2,1,0:T(8,128)} %get-tuple-element.6.a_in, f32[48,48]{1,0:T(8,128)} %get-tuple-element.7.b_in, f32[48,48]{1,0:T(8,128)} %get-tuple-element.8.c_in), custom_call_target="tpu_custom_call" | custom-call | tf_op jit(solution)/shard_map/pallas_call | solution.py:878

commit v7 on v6

--- a/solution.py
+++ b/solution.py
@@ -709,11 +709,11 @@
         return 0
 
     ar_start(1, 1, ar_finish(1, 0))
-    lax.fori_loop(0, 2 * LAST, drain, 0)
     wait_send(sndh, rcvh, hs, hr, (LAST, 0))
     wait_send(sndc, rcvc, cs, cr, (LAST, 0))
     wait_send(sndd, rcvd, ds, dr, ())
     ar_start(2, 1, ar_finish(2, 0))
+    lax.fori_loop(0, 2 * LAST, drain, 0)
     lax.fori_loop(0, 4, drain_coarse, 0)
     wait_send(sndm, rcvm, ms, mr, ())
     for c in both_copies(BP, bs, br) + both_copies(hdcT, ts, tr):

time: 81.1 us -> 81.1 us (level)
  no operation moved by 1% of the time
where the time goes in v7:
time: 81.1 us; the launch traced here: 81 us
  Pallas kernels  80.3 us (99%)
    pallas_call x1, Pallas kernels, shards(): pl.pallas_call(functools.partial(kernel, n_dom, ar_dims), out_shape=(jax....  78.7 us

profile of v7, /device:TPU:1, one launch (start us, length us, event | category | flops | bytes accessed | tf_op | source)
XLA Modules:
  0.0 81.0 jit_solution(10838769303538373705)
XLA Ops:
  0.6 78.7 %shard_map.121 = (f32[16,16,128]{2,1,0:T(8,128)}, f32[48,48]{1,0:T(8,128)}, f32[48,48]{1,0:T(8,128)}) custom-call(f32[16,16,128]{2,1,0:T(8,128)} %x_in.1, f32[16,16,128]{2,1,0:T(8,128)} %p_in.1, f32[4,16,16,128]{3,2,1,0:T(8,128)} %own_in.1, f32[4,16,16,128]{3,2,1,0:T(8,128)} %oth_in.1, f32[16,128]{1,0:T(8,128)} %mass_in.1, s32[4,128]{1,0:T(4,128)} %cols_in.1, ...), custom_call_target="tpu_custom_call" | custom-call | tf_op jit(solution)/shard_map/pallas_call | solution.py:860
  79.4 1.6 %shard_map.122 = (f32[16,16,128]{2,1,0:T(8,128)}, f32[48,48]{1,0:T(8,128)}, f32[48,48]{1,0:T(8,128)}) custom-call(f32[16,16,128]{2,1,0:T(8,128)} %get-tuple-element.6.a_in, f32[48,48]{1,0:T(8,128)} %get-tuple-element.7.b_in, f32[48,48]{1,0:T(8,128)} %get-tuple-element.8.c_in), custom_call_target="tpu_custom_call" | custom-call | tf_op jit(solution)/shard_map/pallas_call | solution.py:878
